TPU v7x, 256 devices: a whole 4x4x8 slice. The times are simulated.
256 devices in a mesh: doc: 128 (over z, x, y), seq: 2 (over core).
Axes of the slice: x: 4, y: 4, z: 8, core: 2. Of those that a mesh axis runs over, the one named last changes fastest.
Arguments:
- queries: bfloat16 [32768, 4096], P(('doc', 'seq')), may hold values from -6 to 6
- vision: bfloat16 [256, 128, 8192], P(None, 'doc', 'seq'), may hold values from -6 to 6
- key_matrix: bfloat16 [8192, 512], P('seq'), may hold values from -0.0625 to 0.0625
- value_matrix: bfloat16 [8192, 512], P('seq'), may hold values from -0.0625 to 0.0625
- query_gain: float32 [128], replicated, may hold values from 0.5 to 1.5
- key_gain: float32 [128], replicated, may hold values from 0.5 to 1.5
- image_count: int32 [128], P('doc'), may hold values from 1 to 8, as said below
- image_slot: int32 [128, 8], replicated, may hold values from -1 to 255, as said below
- image_pos: int32 [128, 8], P('doc'), may hold values from 0 to 256, as said below
- span_end: int32 [128, 8], P('doc'), may hold values from 1 to 256, as said below
Outputs:
- mixed_rows: bfloat16 [32768, 4096], P(('doc', 'seq'))
Inputs may be any that keep to these rules, and one draw needn't show every extreme that they name: `image_count`: the counts sum to 256. For j < image_count[d], image j of document d lies in encoder slot image_slot[d, j]; every slot holds exactly one image; entries with j >= image_count[d] are -1. `image_pos`: non-decreasing in j; 256 for j >= image_count[d]. `span_end`: greater than image_pos for j < image_count[d]; a document's last image is attended to the document's end; 256 for j >= image_count[d].
All inputs are finite; a program needn't handle non-finite values.
Results may differ from a plain program's by a relative error of at most 0.0075.
Values may be sent and summed in bfloat16 or wider, within the bound.
A program may use at most 128 MiB of HBM per device.

v0:
```python
import math

import jax
import jax.numpy as jnp
from jax import lax
from jax.sharding import PartitionSpec as P

HEAD_SIZE = 128
QUERY_HEADS = 32
KEY_VALUE_HEADS = 4
IMG_MAX = 8


epsilon = 1e-05


def head_norm(values, scales):
    mean_square = jnp.mean(values * values, axis=-1, keepdims=True)
    return values * lax.rsqrt(mean_square + epsilon) * scales


def project(block_of_rows, key_matrix, value_matrix):
    matrix = block_of_rows.reshape(-1, block_of_rows.shape[-1])
    key_portion = jnp.dot(matrix, key_matrix, preferred_element_type=jnp.float32)
    value_portion = jnp.dot(matrix, value_matrix, preferred_element_type=jnp.float32)
    matched_pairs = jnp.stack(
        [
            key_portion.reshape(-1, KEY_VALUE_HEADS, HEAD_SIZE),
            value_portion.reshape(-1, KEY_VALUE_HEADS, HEAD_SIZE),
        ],
        axis=2,
    )
    return matched_pairs.reshape(block_of_rows.shape[:-1] + (KEY_VALUE_HEADS * 2 * HEAD_SIZE,))


def finish(matched_pairs, key_gain):
    shaped = matched_pairs.reshape(matched_pairs.shape[:-1] + (-1, 2, HEAD_SIZE))
    normed = head_norm(shaped[..., 0, :], key_gain).astype(jnp.bfloat16)
    value_rows = shaped[..., 1, :].astype(jnp.bfloat16)
    return jnp.stack([normed, value_rows], axis=-2)


def pack_slots(held_rows, image_slot):
    present = image_slot >= 0
    picked = jnp.take(held_rows, jnp.maximum(image_slot, 0), axis=0)
    return jnp.where(present[:, :, None, None], picked, jnp.zeros((), held_rows.dtype))


def shards(
    queries,
    vision,
    key_matrix,
    value_matrix,
    query_gain,
    key_gain,
    image_count,
    image_slot,
    image_pos,
    span_end,
):
    packed = pack_slots(vision, image_slot)
    partial_value = project(
        lax.all_to_all(packed, "doc", split_axis=0, concat_axis=2, tiled=True),
        key_matrix,
        value_matrix,
    )
    summed = lax.psum(partial_value, "seq")
    image_kv = finish(summed[0], key_gain)
    local_tokens = queries.shape[0]
    first_token = lax.axis_index("seq") * local_tokens
    positions = first_token + jnp.arange(local_tokens, dtype=jnp.int32)
    query_head_rows = queries.astype(jnp.float32).reshape(
        local_tokens, KEY_VALUE_HEADS, QUERY_HEADS // KEY_VALUE_HEADS, HEAD_SIZE
    )
    normed_queries = head_norm(query_head_rows, query_gain).astype(jnp.bfloat16)
    live_count = image_count[0]
    slots_seen = jnp.arange(IMG_MAX, dtype=jnp.int32)
    attends = (
        (slots_seen[None, :] < live_count)
        & (image_pos[0][None, :] <= positions[:, None])
        & (positions[:, None] < span_end[0][None, :])
    )
    key_portion = image_kv[:, :, :, 0]
    value_portion = image_kv[:, :, :, 1]
    score_scale = 1.0 / math.sqrt(HEAD_SIZE)
    scores = (
        jnp.einsum(
            "tkgd,jvkd->tkgjv", normed_queries, key_portion, preferred_element_type=jnp.float32
        )
        * score_scale
    )
    weights = jnp.where(attends[:, None, None, :, None], jnp.exp(scores), 0.0).astype(jnp.bfloat16)
    numerator = jnp.einsum(
        "tkgjv,jvkd->tkgd", weights, value_portion, preferred_element_type=jnp.float32
    )
    denominator = jnp.sum(weights, axis=(3, 4), dtype=jnp.float32)
    reached = jnp.any(attends, axis=1)[:, None, None]
    quotient = numerator / jnp.where(reached, denominator, 1.0)[..., None]
    mixed_rows = jnp.where(reached[..., None], quotient, 0.0).astype(jnp.bfloat16)
    return mixed_rows.reshape(local_tokens, QUERY_HEADS * HEAD_SIZE)


def solution(mesh):
    in_specs = (
        P(("doc", "seq"), None),
        P(None, "doc", "seq"),
        P("seq", None),
        P("seq", None),
        P(),
        P(),
        P("doc"),
        P(),
        P("doc", None),
        P("doc", None),
    )
    out_specs = P(("doc", "seq"), None)
    return jax.shard_map(shards, mesh=mesh, in_specs=in_specs, out_specs=out_specs, check_vma=False)
```

profile of v0, /device:TPU:1, one launch (start us, length us, event | category | flops | bytes accessed | tf_op | source)
XLA Modules:
  0.0 312.3 jit_solution(10261297393074261637)
XLA Ops:
  6.5 0.0 copy-start
  6.5 0.8 broadcast_compare_fusion.1
  7.4 0.7 broadcast_maximum_fusion
  8.1 0.1 copy.40
  8.2 0.1 copy.41
  8.3 0.1 copy.42
  8.4 0.1 reshape.162
  8.5 0.0 copy-done
  8.5 7.7 %gather_fusion = bf16[1024,4096]{1,0:T(8,128)(2,1)} fusion(bf16[256,4096]{1,0:T(8,128)(2,1)S(1)} %bitcast.79, s32[1024]{0:T(1024)S(1)} %broadcast_clamp_fusion), kind=kCustom, calls=%fused_computation | custom fusion | bytes 16781312 | tf_op jit(solution)/shard_map/jit(_take)/gather | solution.py:45
  16.3 7.4 %fusion.1 = bf16[128,8,1,4096]{3,1,2,0:T(8,128)(2,1)} fusion(bf16[1024,4096]{1,0:T(8,128)(2,1)} %gather_fusion, pred[128,8]{1,0:T(8,128)(4,1)S(1)} %copy.41, pred[128,8]{1,0:T(8,128)(4,1)S(1)} %copy.40), kind=kLoop, calls=%fused_computation.5 | loop fusion | flops 8388608 | bytes 16779264 | tf_op jit(solution)/shard_map/jit(_where)/select_n | solution.py:46
  23.6 16.9 %all-to-all-start = ((bf16[128,8,1,4096]{3,1,2,0:T(8,128)(2,1)}), bf16[128,8,1,4096]{3,1,2,0:T(8,128)(2,1)}, u32[]{:S(2)}, u32[]{:S(2)}) async-start(bf16[128,8,1,4096]{3,1,2,0:T(8,128)(2,1)} %fusion.1), calls=%async_computation | async-start | bytes 16777216 | tf_op jit(solution)/shard_map/all_to_all | solution.py:63
  40.5 0.2 all-reduce.2.cloned.1.call-start
  40.8 6.4 %copy.60 = bf16[512,4096]{1,0:T(8,128)(2,1)} copy(bf16[512,4096]{0,1:T(8,128)(2,1)} %bitcast.85) | data formatting | bytes 8388608 | tf_op jit(solution)/shard_map/reshape.48
  47.2 6.4 %copy.59 = bf16[512,4096]{1,0:T(8,128)(2,1)} copy(bf16[512,4096]{0,1:T(8,128)(2,1)} %bitcast.86) | data formatting | bytes 8388608 | tf_op jit(solution)/shard_map/reshape.46
  53.6 169.9 %all-to-all-done = bf16[128,8,1,4096]{3,1,2,0:T(8,128)(2,1)} async-done(((bf16[128,8,1,4096]{3,1,2,0:T(8,128)(2,1)}), bf16[128,8,1,4096]{3,1,2,0:T(8,128)(2,1)}, u32[]{:S(2)}, u32[]{:S(2)}) %all-to-all-start) | async-done | bytes 8388640 | tf_op jit(solution)/shard_map/all_to_all | solution.py:63
  223.5 11.3 %copy.44 = bf16[1,8,128,1,4096]{4,2,1,3,0:T(8,128)(2,1)} copy(bf16[1,8,128,1,4096]{4,1,2,3,0:T(8,128)(2,1)} %bitcast.7) | data formatting | bytes 16777216 | tf_op jit(solution)/shard_map/all_to_all | solution.py:63
  234.9 0.0 copy-done.4
  234.9 7.8 %convolution_bitcast_fusion = f32[1024,4,1,128]{3,0,1,2:T(8,128)S(1)} fusion(bf16[1024,4096,1]{1,0,2:T(8,128)(2,1)} %bitcast.83, bf16[4,128,4096]{2,1,0:T(8,128)(2,1)S(1)} %bitcast.88), kind=kOutput, calls=%fused_computation.17 | convolution fusion | flops 4294967296 | bytes 14680064 | tf_op jit(solution)/shard_map/dot_general | solution.py:25
  242.7 0.0 copy-done.2
  242.7 0.0 copy-done.3
  242.7 4.5 %convolution_bitcast_fusion.1 = f32[1024,4,1,128]{3,0,1,2:T(8,128)S(1)} fusion(bf16[1024,4096,1]{1,0,2:T(8,128)(2,1)S(1)} %bitcast.84, bf16[4,128,4096]{2,1,0:T(8,128)(2,1)S(1)} %bitcast.87), kind=kOutput, calls=%fused_computation.18 | convolution fusion | flops 4294967296 | bytes 14680064 | tf_op jit(solution)/shard_map/dot_general | solution.py:24
  247.3 2.2 pad_maximum_fusion
  249.5 5.4 %copy.47 = f32[8,128,4,2,128]{1,4,0,2,3:T(8,128)} copy(f32[8,128,4,2,128]{4,1,0,2,3:T(8,128)} %bitcast.82) | data formatting | bytes 8388608 | tf_op jit(solution)/shard_map/reshape;squeeze | solution.py:37
  254.9 0.0 all-reduce.2.cloned.1.call-update
  254.9 1.2 copy-done.5
  256.1 0.2 convert_bitcast_fusion
  256.3 0.0 copy-start.8
  256.3 0.0 copy-start.9
  256.3 0.0 copy-start.7
  256.3 0.4 copy.66
  256.7 0.0 copy-start.10
  256.7 0.8 multiply_reduce_fusion
  257.5 0.1 copy.48
  257.7 0.2 copy.49
  258.5 0.0 copy-done.8
  258.5 0.0 copy-done.9
  258.5 0.1 fusion.12
  258.6 0.0 copy-done.7
  258.6 0.7 fusion.6
  259.3 34.8 %all-reduce.2.cloned.1.call-done = f32[8,128,4,2,128]{1,4,0,2,3:T(8,128)} async-done(((f32[8,128,4,2,128]{1,4,0,2,3:T(8,128)}), f32[8,128,4,2,128]{1,4,0,2,3:T(8,128)}) %all-reduce.2.cloned.1.call-update) | async-done | bytes 4194320 | tf_op jit(solution)/shard_map/psum | solution.py:67
  294.2 1.8 multiply_reduce_fusion.1
  295.9 0.0 copy-done.10
  296.0 0.0 copy-start.6
  296.0 6.8 %convert_reduce_fusion = (f32[128,4,8]{0,2,1:T(8,128)S(1)}, bf16[128,4,8,8,128]{0,4,2,3,1:T(8,128)(2,1)S(1)}) fusion(bf16[128,4,8,128,1]{3,2,1,0,4:T(8,128)(2,1)S(1)} %fusion.6, f32[8,128,4,2,128]{1,4,0,2,3:T(8,128)} %all-reduce.2.cloned.1.call-done, f32[128]{0:T(128)S(1)} %copy-done.10, f32[8,128,4]{1,0,2:T(8,128)S(1)} %add_rsqrt_fusion.1, ...), kind=kOutput, calls=%fused_computation.3 | convolution fusion | flops 1096282112 | bytes 11568640 | tf_op jit(solution)/shard_map/tkgd,jvkd->tkgjv/dot_general | solution.py:87
  302.8 0.0 copy-start.1
  302.8 1.3 fusion.3
  304.2 1.3 copy.53
  305.5 0.0 copy-done.1
  (11 shorter events, 0.1 us)
Async XLA Ops:
  6.5 2.0 copy-start
  23.6 199.9 %all-to-all-start = ((bf16[128,8,1,4096]{3,1,2,0:T(8,128)(2,1)}), bf16[128,8,1,4096]{3,1,2,0:T(8,128)(2,1)}, u32[]{:S(2)}, u32[]{:S(2)}) async-start(bf16[128,8,1,4096]{3,1,2,0:T(8,128)(2,1)} %fusion.1), calls=%async_computation | async-start | bytes 16777216 | tf_op jit(solution)/shard_map/all_to_all | solution.py:63
  40.5 253.6 %all-reduce.2.cloned.1.call-start = ((), (), s32[]{:S(2)}) async-start(), calls=%async_computation.1 | async-start | bytes 8388608 | tf_op jit(solution)/shard_map/psum | solution.py:67
  223.5 11.3 %copy-start.4 = (bf16[512,4096]{1,0:T(8,128)(2,1)S(1)}, bf16[512,4096]{1,0:T(8,128)(2,1)}, u32[]{:S(2)}) copy-start(bf16[512,4096]{1,0:T(8,128)(2,1)} %copy.60) | copy-start | bytes 12582916
  234.9 7.8 %copy-start.2 = (bf16[1,8,128,1,4096]{4,2,1,3,0:T(8,128)(2,1)S(1)}, bf16[1,8,128,1,4096]{4,2,1,3,0:T(8,128)(2,1)}, u32[]{:S(2)}) copy-start(bf16[1,8,128,1,4096]{4,2,1,3,0:T(8,128)(2,1)} %copy.44) | copy-start | bytes 25165828
  234.9 7.9 %copy-start.3 = (bf16[512,4096]{1,0:T(8,128)(2,1)S(1)}, bf16[512,4096]{1,0:T(8,128)(2,1)}, u32[]{:S(2)}) copy-start(bf16[512,4096]{1,0:T(8,128)(2,1)} %copy.59) | copy-start | bytes 12582916
  254.9 1.2 copy-start.5
  256.3 2.2 copy-start.8
  256.3 2.2 copy-start.9
  256.3 2.3 copy-start.7
  256.7 39.2 %copy-start.10 = (f32[128]{0:T(128)S(1)}, f32[128]{0:T(128)}, u32[]{:S(2)}) copy-start(f32[128]{0:T(128)} %param.15) | copy-start | bytes 1540
  296.0 6.9 %copy-start.6 = (f32[8,128,4,2,128]{1,4,0,2,3:T(8,128)S(1)}, f32[8,128,4,2,128]{1,4,0,2,3:T(8,128)}, u32[]{:S(2)}) copy-start(f32[8,128,4,2,128]{1,4,0,2,3:T(8,128)} %all-reduce.2.cloned.1.call-done) | copy-start | bytes 12582916
  302.8 2.7 copy-start.1
Sparse Core Ops, SparseCore 0:
  255.0 39.0 all-reduce.1
where the time goes:
time: 313 us; the launch traced here: 312 us
  waiting for transfers between devices  205 us (65%)
  local copies, waits for them, and re-layouts  40.9 us (13%)
  matrix products  20.5 us (7%)
  starting transfers between devices  17.1 us (5%)
  other arithmetic  14.8 us (5%)
  between operations  14.3 us (5%)
    all_to_all x1, waiting for transfers between devices, shards(): lax.all_to_all(packed, 'doc', split_axis=0, concat_axis=2, tiled=True)  170 us
    psum x1, waiting for transfers between devices, shards(): summed = lax.psum(partial_value, 'seq')  34.8 us
    all_to_all x1, starting transfers between devices, shards(): lax.all_to_all(packed, 'doc', split_axis=0, concat_axis=2, tiled=True)  16.9 us
    another operation x2, local copies, waits for them, and re-layouts  12.9 us
    all_to_all x1, local copies, waits for them, and re-layouts, shards(): lax.all_to_all(packed, 'doc', split_axis=0, concat_axis=2, tiled=True)  11.3 us
    dot_general x1, matrix products, project(): jnp.dot(matrix, value_matrix, preferred_element_type=jnp.float32)  7.84 us
    gather x1, local copies, waits for them, and re-layouts, pack_slots(): picked = jnp.take(held_rows, jnp.maximum(image_slot, 0), axis=0)  7.73 us
    select_n x1, other arithmetic, pack_slots(): jnp.where(present[:, :, None, None], picked, jnp.zeros((), held_rows.dtype))  7.38 us
  transfers between devices with their start and end apart: 2, of which 2 were waited for; matrix products, arithmetic and copies ran while one was open for 5% of the time, Pallas kernels for 0%

commit v1 on v0

v1 whole, which is shorter than its diff:
```python
import math

import jax
import jax.numpy as jnp
from jax import lax
from jax.sharding import PartitionSpec as P

HEAD_SIZE = 128
QUERY_HEADS = 32
KEY_VALUE_HEADS = 4
IMG_MAX = 8


epsilon = 1e-05


def head_norm(values, scales):
    mean_square = jnp.mean(values * values, axis=-1, keepdims=True)
    return values * lax.rsqrt(mean_square + epsilon) * scales


def shards(
    queries,
    vision,
    key_matrix,
    value_matrix,
    query_gain,
    key_gain,
    image_count,
    image_slot,
    image_pos,
    span_end,
):
    n_slots = vision.shape[0]
    core = lax.axis_index("seq")
    rows = vision.reshape(n_slots, -1)
    keys = jnp.dot(rows, key_matrix, preferred_element_type=jnp.float32)
    values = jnp.dot(rows, value_matrix, preferred_element_type=jnp.float32)
    half = keys.shape[1] // 2
    other = [(0, 1), (1, 0)]

    def pick(c):
        start = c * half
        return jnp.concatenate(
            [lax.dynamic_slice_in_dim(keys, start, half, 1), lax.dynamic_slice_in_dim(values, start, half, 1)], axis=1
        )

    mine = pick(core) + lax.ppermute(pick(1 - core), "seq", other)
    mine = mine.reshape(n_slots, 2, 2, HEAD_SIZE)
    kv = jnp.concatenate(
        [head_norm(mine[:, 0], key_gain).astype(jnp.bfloat16), mine[:, 1].astype(jnp.bfloat16)], axis=1
    ).reshape(n_slots, 4 * HEAD_SIZE)
    slots = image_slot.reshape(-1)
    one_hot = (slots[:, None] == jnp.arange(n_slots, dtype=jnp.int32)[None, :]).astype(jnp.bfloat16)
    packed = jnp.dot(one_hot, kv, preferred_element_type=jnp.float32).astype(jnp.bfloat16)
    packed = packed.reshape(image_slot.shape[0], IMG_MAX * 4 * HEAD_SIZE)
    got = lax.all_to_all(packed, "doc", split_axis=0, concat_axis=0, tiled=True)
    theirs = lax.ppermute(got, "seq", other)
    first = jnp.where(core == 0, got, theirs).reshape(-1, IMG_MAX, 2, 2, HEAD_SIZE)
    second = jnp.where(core == 0, theirs, got).reshape(-1, IMG_MAX, 2, 2, HEAD_SIZE)
    both = jnp.concatenate([first, second], axis=3)
    n_keys = both.shape[0] * IMG_MAX
    both = both.reshape(n_keys, 2, KEY_VALUE_HEADS, HEAD_SIZE)
    local_tokens = queries.shape[0]
    positions = core * local_tokens + jnp.arange(local_tokens, dtype=jnp.int32)
    q = queries.astype(jnp.float32).reshape(local_tokens, KEY_VALUE_HEADS, QUERY_HEADS // KEY_VALUE_HEADS, HEAD_SIZE)
    q = head_norm(q, query_gain).astype(jnp.bfloat16)
    seen = jnp.arange(IMG_MAX, dtype=jnp.int32)
    attends = (
        (seen[None, :] < image_count[0])
        & (image_pos[0][None, :] <= positions[:, None])
        & (positions[:, None] < span_end[0][None, :])
    )
    scores = jnp.einsum("tkgd,nkd->tkgn", q, both[:, 0], preferred_element_type=jnp.float32)
    scores = scores * (1.0 / math.sqrt(HEAD_SIZE))
    key_mask = jnp.tile(attends, (1, n_keys // IMG_MAX))
    weights = jnp.where(key_mask[:, None, None, :], jnp.exp(scores), 0.0).astype(jnp.bfloat16)
    numerator = jnp.einsum("tkgn,nkd->tkgd", weights, both[:, 1], preferred_element_type=jnp.float32)
    denominator = jnp.sum(weights, axis=3, dtype=jnp.float32)
    reached = jnp.any(attends, axis=1)[:, None, None]
    quotient = numerator / jnp.where(reached, denominator, 1.0)[..., None]
    mixed_rows = jnp.where(reached[..., None], quotient, 0.0).astype(jnp.bfloat16)
    return mixed_rows.reshape(local_tokens, QUERY_HEADS * HEAD_SIZE)


def solution(mesh):
    in_specs = (
        P(("doc", "seq"), None),
        P(None, "doc", "seq"),
        P("seq", None),
        P("seq", None),
        P(),
        P(),
        P("doc"),
        P(),
        P("doc", None),
        P("doc", None),
    )
    out_specs = P(("doc", "seq"), None)
    return jax.shard_map(shards, mesh=mesh, in_specs=in_specs, out_specs=out_specs, check_vma=False)
```

time: 313 us -> 103 us (0.33)
  waiting for transfers between devices: 205 us -> 26.3 us
  local copies, waits for them, and re-layouts: 40.9 us -> 25.1 us
  between operations: 14.3 us -> 0.92 us
  matrix products: 20.5 us -> 12.2 us
    all_to_all x1, waiting for transfers between devices: 170 us -> 24.2 us  [shards(): got = lax.all_to_all(packed, 'doc', split_axis=0, concat_axis=0, tiled=True)]
    psum x1 -> x0, waiting for transfers between devices: 34.8 us -> none  [shards(): summed = lax.psum(partial_value, 'seq')]
    another operation x3 -> x1, local copies, waits for them, and re-layouts: 18.2 us -> 0.03 us  [shards(): key_mask = jnp.tile(attends, (1, n_keys // IMG_MAX))]
    unnamed x23 -> x30, local copies, waits for them, and re-layouts: 1.62 us -> 13.6 us
    all_to_all x0 -> x1, other arithmetic: none -> 8.38 us  [shards(): got = lax.all_to_all(packed, 'doc', split_axis=0, concat_axis=0, tiled=True)]
    dot_general x4 -> x5, matrix products: 20.5 us -> 12.2 us  [the longest x1 4.64 us: shards(): jnp.einsum('tkgd,nkd->tkgn', q, both[:, 0], preferred_element_type=jnp.fl...]
    gather x1 -> x0, local copies, waits for them, and re-layouts: 7.73 us -> none  [pack_slots(): picked = jnp.take(held_rows, jnp.maximum(image_slot, 0), axis=0)]
    all_to_all x1 -> x2, local copies, waits for them, and re-layouts: 11.3 us -> 3.67 us  [shards(): got = lax.all_to_all(packed, 'doc', split_axis=0, concat_axis=0, tiled=True)]
  transfers between devices with their start and end apart: 2 -> 3, of which waited for: 2 -> 3; matrix products, arithmetic and copies ran while one was open for 5% -> 5% of each run, Pallas kernels for 0% -> 0%
where the time goes in v1:
time: 103 us; the launch traced here: 102 us
  waiting for transfers between devices  26.3 us (26%)
  local copies, waits for them, and re-layouts  25.1 us (24%)
  starting transfers between devices  20.2 us (20%)
  other arithmetic  17.7 us (17%)
  matrix products  12.2 us (12%)
    all_to_all x1, waiting for transfers between devices, shards(): got = lax.all_to_all(packed, 'doc', split_axis=0, concat_axis=0, tiled=True)  24.2 us
    all_to_all x1, starting transfers between devices, shards(): got = lax.all_to_all(packed, 'doc', split_axis=0, concat_axis=0, tiled=True)  13.8 us
    unnamed x30, local copies, waits for them, and re-layouts  13.6 us
    all_to_all x1, other arithmetic, shards(): got = lax.all_to_all(packed, 'doc', split_axis=0, concat_axis=0, tiled=True)  8.38 us
    dot_general x1, matrix products, shards(): jnp.einsum('tkgd,nkd->tkgn', q, both[:, 0], preferred_element_type=jnp.fl...  4.64 us
    concatenate x3, local copies, waits for them, and re-layouts, shards(): both = jnp.concatenate([first, second], axis=3)  4.61 us
    all_to_all x2, local copies, waits for them, and re-layouts, shards(): got = lax.all_to_all(packed, 'doc', split_axis=0, concat_axis=0, tiled=True)  3.67 us
    dot_general x1, matrix products, shards(): keys = jnp.dot(rows, key_matrix, preferred_element_type=jnp.float32)  3.57 us
  transfers between devices with their start and end apart: 3, of which 3 were waited for; matrix products, arithmetic and copies ran while one was open for 5% of the time, Pallas kernels for 0%

profile of v1, /device:TPU:1, one launch (start us, length us, event | category | flops | bytes accessed | tf_op | source)
XLA Modules:
  0.0 102.4 jit_solution(17480816889411110368)
XLA Ops:
  0.0 0.0 copy-start
  0.0 1.6 %copy-done = bf16[256,1,4096]{2,0,1:T(8,128)(2,1)S(1)} copy-done((bf16[256,1,4096]{2,0,1:T(8,128)(2,1)S(1)}, bf16[256,1,4096]{2,0,1:T(8,128)(2,1)}, u32[]{:S(2)}) %copy-start) | copy-done | bytes 2097176
  1.6 3.6 %fusion.5 = f32[256,512]{1,0:T(8,128)S(1)} fusion(bf16[4096,512]{1,0:T(8,128)(2,1)} %param.12, bf16[256,1,4096]{2,0,1:T(8,128)(2,1)S(1)} %copy-done), kind=kOutput, calls=%fused_computation.8 | convolution fusion | flops 1073741824 | bytes 6815744 | tf_op jit(solution)/shard_map/dot_general | solution.py:37
  5.2 0.0 copy-done.11
  5.2 2.1 %fusion.3 = f32[256,512]{1,0:T(8,128)} fusion(bf16[4096,512]{1,0:T(8,128)(2,1)S(1)} %copy-done.11, bf16[256,1,4096]{2,0,1:T(8,128)(2,1)S(1)} %copy-done), kind=kOutput, calls=%fused_computation.6 | convolution fusion | flops 1073741824 | bytes 6815744 | tf_op jit(solution)/shard_map/dot_general | solution.py:38
  7.3 1.1 %constant_dynamic-slice_fusion.2 = (f32[256,256]{1,0:T(8,128)S(1)}, f32[256,256]{1,0:T(8,128)S(1)}, f32[256,256]{1,0:T(8,128)S(1)}, f32[256,256]{1,0:T(8,128)S(1)}) fusion(f32[256,512]{1,0:T(8,128)} %fusion.3, s32[]{:T(128)S(6)} %select_n.37, s32[]{:T(128)S(6)} %select_n.38, f32[256,512]{1,0:T(8,128)S(1)} %fusion.5), kind=kLoop, calls=%fused_computation.41 | loop fusion | bytes 2097160 | tf_op jit(solution)/shard_map/dynamic_slice | solution.py:45
  8.4 0.9 pad_maximum_fusion
  9.3 3.2 %collective-permute-start = (f32[256,512]{1,0:T(8,128)}, f32[256,512]{1,0:T(8,128)S(1)}, u32[]{:S(2)}, u32[]{:S(2)}) collective-permute-start(f32[256,512]{1,0:T(8,128)} %pad_maximum_fusion), channel_id=1, source_target_pairs={{0,1},{1,0},{2,3},{3,2},{4,5},{5,4},{6,7},{7,6},{8,9},{9,8},{10,11... | collective-permute-start | bytes 1572872 | tf_op jit(solution)/shard_map/ppermute | solution.py:48
  12.5 0.0 copy-done.6
  12.5 0.1 copy.54
  12.6 0.1 eq.20
  12.7 1.6 %collective-permute-done = f32[256,512]{1,0:T(8,128)S(1)} collective-permute-done((f32[256,512]{1,0:T(8,128)}, f32[256,512]{1,0:T(8,128)S(1)}, u32[]{:S(2)}, u32[]{:S(2)}) %collective-permute-start) | collective-permute-done | bytes 524320 | tf_op jit(solution)/shard_map/ppermute | solution.py:48
  14.3 0.8 copy-done.5
  15.1 1.1 %maximum_add_fusion = f32[256,512]{1,0:T(8,128)S(1)} fusion(f32[256,512]{1,0:T(8,128)} %copy-done.5, f32[256,256]{1,0:T(8,128)S(1)} %get-tuple-element.11, f32[256,256]{1,0:T(8,128)S(1)} %get-tuple-element.16), kind=kLoop, calls=%fused_computation.23 | loop fusion | flops 262144 | bytes 1572864 | tf_op jit(solution)/shard_map/add | solution.py:48
  16.2 0.3 reshape.139
  16.5 0.3 multiply_reduce_fusion.1
  16.9 0.1 fusion.11
  17.0 0.0 copy-done.7
  17.0 0.3 multiply_convert_fusion.1
  17.4 0.3 pad_maximum_fusion.1
  17.7 0.5 convolution_convert_fusion
  18.1 3.2 %all_to_all.11 = bf16[128,1,4096]{2,1,0:T(2,128)(2,1)} reshape(bf16[1024,512]{1,0:T(8,128)(2,1)S(1)} %convolution_convert_fusion) | data formatting | bytes 2097152 | tf_op jit(solution)/shard_map/all_to_all | solution.py:57
  21.3 0.5 broadcast.103
  21.8 8.4 %reduce = bf16[128,4096]{1,0:T(8,128)(2,1)S(1)} reduce(bf16[128,1,4096]{2,1,0:T(2,128)(2,1)} %all_to_all.11, bf16[]{:T(256)} %broadcast.103), dimensions={1}, to_apply=%all_to_all.11.reduce_sub_computation | reduce | bytes 2097154 | tf_op jit(solution)/shard_map/all_to_all | solution.py:57
  30.2 1.6 %reshape.149 = bf16[128,2,2048]{2,1,0:T(2,128)(2,1)} reshape(bf16[128,4096]{1,0:T(8,128)(2,1)S(1)} %reduce) | data formatting | bytes 2097152
  31.8 13.8 %all-to-all-start = ((bf16[128,2,2048]{2,1,0:T(2,128)(2,1)}), bf16[128,2,2048]{2,1,0:T(2,128)(2,1)S(1)}, u32[]{:S(2)}, u32[]{:S(2)}) async-start(bf16[128,2,2048]{2,1,0:T(2,128)(2,1)} %reshape.149), calls=%async_computation | async-start | bytes 2097152 | tf_op jit(solution)/shard_map/all_to_all | solution.py:57
  46.2 1.4 %convert_bitcast_fusion = f32[16,8,32,128]{3,1,2,0:T(8,128)S(1)} fusion(bf16[128,4096]{1,0:T(8,128)(2,1)} %param.10), kind=kLoop, calls=%fused_computation.10 | loop fusion | flops 524288 | bytes 3145728
  47.6 0.4 copy.77
  48.0 0.0 copy-start.2
  48.0 1.3 %copy-done.2 = f32[16,8,32,128]{3,2,1,0:T(8,128)} copy-done((f32[16,8,32,128]{3,2,1,0:T(8,128)}, f32[16,8,32,128]{3,2,1,0:T(8,128)S(1)}, u32[]{:S(2)}) %copy-start.2) | copy-done | bytes 2097176
  49.4 0.8 multiply_reduce_fusion
  50.2 0.1 copy.62
  50.3 0.2 copy.63
  50.5 24.2 %all-to-all-done = bf16[128,2,2048]{2,1,0:T(2,128)(2,1)S(1)} async-done(((bf16[128,2,2048]{2,1,0:T(2,128)(2,1)}), bf16[128,2,2048]{2,1,0:T(2,128)(2,1)S(1)}, u32[]{:S(2)}, u32[]{:S(2)}) %all-to-all-start) | async-done | bytes 1048608 | tf_op jit(solution)/shard_map/all_to_all | solution.py:57
  74.7 3.4 %reshape.150 = bf16[128,1,4096]{2,1,0:T(2,128)(2,1)} reshape(bf16[128,2,2048]{2,1,0:T(2,128)(2,1)S(1)} %all-to-all-done) | data formatting | bytes 2097152
  78.1 2.9 %copy.100 = bf16[128,1,4096]{2,0,1:T(8,128)(2,1)S(1)} copy(bf16[128,1,4096]{2,1,0:T(2,128)(2,1)} %reshape.150) | data formatting | bytes 2097152
  81.0 3.2 %collective-permute-start.1 = (bf16[128,4096]{1,0:T(8,128)(2,1)S(1)}, bf16[128,4096]{1,0:T(8,128)(2,1)S(1)}, u32[]{:S(2)}, u32[]{:S(2)}) collective-permute-start(bf16[128,4096]{1,0:T(8,128)(2,1)S(1)} %bitcast.63), channel_id=1, source_target_pairs={{0,1},{1,0},{2,3},{3,2},{4,5},{5,4},{6,7},{7,6},{8,9},{9,8},{10,11... | collective-permute-start | bytes 3145736 | tf_op jit(solution)/shard_map/ppermute | solution.py:58
  84.2 0.1 fusion.12
  84.3 1.5 %multiply_convert_fusion = bf16[128,4,8,128]{3,2,1,0:T(8,128)(2,1)} fusion(f32[128,4,8,128]{3,2,1,0:T(8,128)S(1)} %bitcast.62, f32[128]{0:T(128)S(1)} %copy-done.8, f32[128,4,8]{2,1,0:T(4,128)S(1)} %copy.63), kind=kLoop, calls=%fused_computation.11 | loop fusion | flops 1572864 | bytes 3162624 | tf_op jit(solution)/shard_map/convert_element_type | solution.py:67
  85.8 0.6 collective-permute-done.1
  86.4 2.5 %broadcast_select_fusion = (bf16[128,4096]{1,0:T(8,128)(2,1)}, bf16[128,4096]{1,0:T(8,128)(2,1)}) fusion(bf16[128,4096]{1,0:T(8,128)(2,1)S(1)} %collective-permute-done.1, pred[]{:T(512)S(6)} %eq.19, bf16[128,1,4096]{2,1,0:T(2,128)(2,1)S(1)} %copy-done.1), kind=kLoop, calls=%fused_computation.21 | loop fusion | flops 1048576 | bytes 4194305 | tf_op jit(solution)/shard_map/jit(_where)/select_n | solution.py:60
  88.9 1.8 %concatenate.21 = bf16[1024,2,2,128]{3,2,1,0:T(2,128)(2,1)S(1)} reshape(bf16[128,4096]{1,0:T(8,128)(2,1)} %get-tuple-element.7) | data formatting | bytes 2097152 | tf_op jit(solution)/shard_map/concatenate | solution.py:61
  90.7 2.6 %concatenate.20 = bf16[1024,2,2,128]{3,2,1,0:T(2,128)(2,1)} reshape(bf16[128,4096]{1,0:T(8,128)(2,1)} %get-tuple-element.8) | data formatting | bytes 2097152 | tf_op jit(solution)/shard_map/concatenate | solution.py:61
  93.3 1.4 %copy_dynamic-update-slice_fusion.1 = bf16[1024,2,4,128]{3,0,2,1:T(8,128)(2,1)S(1)} fusion(bf16[1024,2,2,128]{3,2,1,0:T(2,128)(2,1)} %concatenate.20), kind=kLoop, calls=%fused_computation.19 | loop fusion | bytes 2097152
  94.7 0.3 copy_dynamic-update-slice_fusion
  95.0 4.6 %convert_reduce_fusion = (f32[128,4,8]{0,2,1:T(8,128)S(1)}, bf16[128,4,8,1024]{0,3,2,1:T(8,128)(2,1)S(1)}) fusion(bf16[128,4,8,128]{3,2,1,0:T(8,128)(2,1)S(1)} %copy-done.4, bf16[1024,2,4,128]{3,0,2,1:T(8,128)(2,1)S(1)} %copy_dynamic-update-slice_fusion, pred[128,1024]{0,1:T(8,128)(4,1)S(1)} %broadcast_bitcast_fusion), kind=kOutput, calls=%fused_computation.2 | convolution fusion | flops 1094709248 | bytes 10633216 | tf_op jit(solution)/shard_map/tkgd,nkd->tkgn/dot_general | solution.py:74
  99.7 1.4 %fusion.2 = bf16[128,4,8,128]{0,3,2,1:T(8,128)(2,1)S(1)} fusion(bf16[128,4,8,1024]{0,3,2,1:T(8,128)(2,1)S(1)} %get-tuple-element.14, bf16[1024,2,4,128]{3,0,2,1:T(8,128)(2,1)S(1)} %copy_dynamic-update-slice_fusion, f32[128,4,8]{0,2,1:T(8,128)S(1)} %broadcast_select_fusion.2, pred[128]{0:T(512)(128)(4,1)S(1)} %get-tuple-element.5), kind=kOutput, calls=%fused_computation.5 | convolution fusion | flops 1075314688 | bytes 10502656 | tf_op jit(solution)/shard_map/tkgn,nkd->tkgd/dot_general | solution.py:78
  101.0 1.3 %copy.67 = bf16[128,4096]{1,0:T(8,128)(2,1)} copy(bf16[128,4096]{0,1:T(8,128)(2,1)S(1)} %bitcast.65) | data formatting | bytes 2097152 | tf_op jit(solution)/shard_map/reshape | solution.py:83
  (22 shorter events, 0.1 us)
Async XLA Ops:
  0.0 1.6 %copy-start = (bf16[256,1,4096]{2,0,1:T(8,128)(2,1)S(1)}, bf16[256,1,4096]{2,0,1:T(8,128)(2,1)}, u32[]{:S(2)}) copy-start(bf16[256,1,4096]{2,0,1:T(8,128)(2,1)} %param.11) | copy-start | bytes 6291460
  1.6 3.6 %copy-start.11 = (bf16[4096,512]{1,0:T(8,128)(2,1)S(1)}, bf16[4096,512]{1,0:T(8,128)(2,1)}, u32[]{:S(2)}) copy-start(bf16[4096,512]{1,0:T(8,128)(2,1)} %param.13) | copy-start | bytes 12582916
  7.3 5.2 %copy-start.6 = (s32[128,8]{0,1:T(8,128)S(1)}, s32[128,8]{0,1:T(8,128)}, u32[]{:S(2)}) copy-start(s32[128,8]{0,1:T(8,128)} %param.17) | copy-start | bytes 12292
  9.3 7.7 %copy-start.7 = (f32[128]{0:T(128)S(1)}, f32[128]{0:T(128)}, u32[]{:S(2)}) copy-start(f32[128]{0:T(128)} %param.15) | copy-start | bytes 1540
  9.3 5.0 %collective-permute-start = (f32[256,512]{1,0:T(8,128)}, f32[256,512]{1,0:T(8,128)S(1)}, u32[]{:S(2)}, u32[]{:S(2)}) collective-permute-start(f32[256,512]{1,0:T(8,128)} %pad_maximum_fusion), channel_id=1, source_target_pairs={{0,1},{1,0},{2,3},{3,2},{4,5},{5,4},{6,7},{7,6},{8,9},{9,8},{10,11... | collective-permute-start | bytes 1572872 | tf_op jit(solution)/shard_map/ppermute | solution.py:48
  14.3 0.8 copy-start.5
  31.8 42.9 %all-to-all-start = ((bf16[128,2,2048]{2,1,0:T(2,128)(2,1)}), bf16[128,2,2048]{2,1,0:T(2,128)(2,1)S(1)}, u32[]{:S(2)}, u32[]{:S(2)}) async-start(bf16[128,2,2048]{2,1,0:T(2,128)(2,1)} %reshape.149), calls=%async_computation | async-start | bytes 2097152 | tf_op jit(solution)/shard_map/all_to_all | solution.py:57
  48.0 1.3 %copy-start.2 = (f32[16,8,32,128]{3,2,1,0:T(8,128)}, f32[16,8,32,128]{3,2,1,0:T(8,128)S(1)}, u32[]{:S(2)}) copy-start(f32[16,8,32,128]{3,2,1,0:T(8,128)S(1)} %copy.77) | copy-start | bytes 6291460
  78.1 6.1 %copy-start.9 = (s32[1,8]{1,0:T(1,128)S(1)}, s32[1,8]{1,0:T(1,128)}, u32[]{:S(2)}) copy-start(s32[1,8]{1,0:T(1,128)} %param.19) | copy-start | bytes 100
  78.1 6.1 %copy-start.10 = (s32[1,8]{1,0:T(1,128)S(1)}, s32[1,8]{1,0:T(1,128)}, u32[]{:S(2)}) copy-start(s32[1,8]{1,0:T(1,128)} %param.18) | copy-start | bytes 100
  78.1 6.2 %copy-start.3 = (f32[16,8,32,128]{3,2,1,0:T(8,128)S(1)}, f32[16,8,32,128]{3,2,1,0:T(8,128)}, u32[]{:S(2)}) copy-start(f32[16,8,32,128]{3,2,1,0:T(8,128)} %copy-done.2) | copy-start | bytes 6291460
  78.1 6.2 %copy-start.8 = (f32[128]{0:T(128)S(1)}, f32[128]{0:T(128)}, u32[]{:S(2)}) copy-start(f32[128]{0:T(128)} %param.14) | copy-start | bytes 1540
  81.0 5.5 %copy-start.1 = (bf16[128,1,4096]{2,1,0:T(2,128)(2,1)S(1)}, bf16[128,1,4096]{2,1,0:T(2,128)(2,1)}, u32[]{:S(2)}) copy-start(bf16[128,1,4096]{2,1,0:T(2,128)(2,1)} %reshape.150) | copy-start | bytes 3145732
  81.0 5.4 %collective-permute-start.1 = (bf16[128,4096]{1,0:T(8,128)(2,1)S(1)}, bf16[128,4096]{1,0:T(8,128)(2,1)S(1)}, u32[]{:S(2)}, u32[]{:S(2)}) collective-permute-start(bf16[128,4096]{1,0:T(8,128)(2,1)S(1)} %bitcast.63), channel_id=1, source_target_pairs={{0,1},{1,0},{2,3},{3,2},{4,5},{5,4},{6,7},{7,6},{8,9},{9,8},{10,11... | collective-permute-start | bytes 3145736 | tf_op jit(solution)/shard_map/ppermute | solution.py:58
  93.3 1.7 %copy-start.4 = (bf16[128,4,8,128]{3,2,1,0:T(8,128)(2,1)S(1)}, bf16[128,4,8,128]{3,2,1,0:T(8,128)(2,1)}, u32[]{:S(2)}) copy-start(bf16[128,4,8,128]{3,2,1,0:T(8,128)(2,1)} %multiply_convert_fusion) | copy-start | bytes 3145732

commit v2 on v1

--- a/solution.py
+++ b/solution.py
@@ -1,15 +1,23 @@
+import functools
 import math
 
 import jax
 import jax.numpy as jnp
 from jax import lax
+from jax.experimental import pallas as pl
+from jax.experimental.pallas import tpu as pltpu
 from jax.sharding import PartitionSpec as P
 
 HEAD_SIZE = 128
 QUERY_HEADS = 32
 KEY_VALUE_HEADS = 4
 IMG_MAX = 8
-
+GROUP = QUERY_HEADS // KEY_VALUE_HEADS
+PLANE = 16
+PLANES = 8
+CAPACITY = 48
+MESH = pl.DeviceIdType.MESH
+MASKED = -32768.0
 
 epsilon = 1e-05
 
@@ -19,7 +27,7 @@
     return values * lax.rsqrt(mean_square + epsilon) * scales
 
 
-def shards(
+def general_route(
     queries,
     vision,
     key_matrix,
@@ -63,7 +71,7 @@
     both = both.reshape(n_keys, 2, KEY_VALUE_HEADS, HEAD_SIZE)
     local_tokens = queries.shape[0]
     positions = core * local_tokens + jnp.arange(local_tokens, dtype=jnp.int32)
-    q = queries.astype(jnp.float32).reshape(local_tokens, KEY_VALUE_HEADS, QUERY_HEADS // KEY_VALUE_HEADS, HEAD_SIZE)
+    q = queries.astype(jnp.float32).reshape(local_tokens, KEY_VALUE_HEADS, GROUP, HEAD_SIZE)
     q = head_norm(q, query_gain).astype(jnp.bfloat16)
     seen = jnp.arange(IMG_MAX, dtype=jnp.int32)
     attends = (
@@ -83,6 +91,448 @@
     return mixed_rows.reshape(local_tokens, QUERY_HEADS * HEAD_SIZE)
 
 
+def iota(shape, axis):
+    return lax.broadcasted_iota(jnp.int32, shape, axis)
+
+
+def flag(condition):
+    return condition.astype(jnp.float32).astype(jnp.bfloat16)
+
+
+def mm(a, b, contract=((1,), (0,))):
+    return lax.dot_general(a, b, (contract, ((), ())), preferred_element_type=jnp.float32)
+
+
+RIGHT = ((1,), (1,))
+
+
+def fused_kernel(
+    q_hbm,
+    x_hbm,
+    wk_hbm,
+    wv_hbm,
+    qg_ref,
+    kg_ref,
+    count_ref,
+    slot_ref,
+    pos_ref,
+    end_ref,
+    out_hbm,
+    q_v,
+    x_v,
+    w_v,
+    part_send,
+    part_recv,
+    part_mine,
+    pick1,
+    expand,
+    send1,
+    recv1,
+    send2,
+    recv2,
+    q_send,
+    q_all,
+    k_tail,
+    o_v,
+    o_send,
+    local_sem,
+    w_sem,
+    out_sem,
+    part_sems,
+    q_sems,
+    o_sems,
+    s1_sem,
+    r1_sem,
+    s2_sem,
+    r2_sem,
+):
+    doc = lax.axis_index("doc")
+    core = lax.axis_index("seq")
+    sibling = 1 - core
+    z, p = doc // PLANE, doc % PLANE
+    px, py = p // 4, p % 4
+    tokens = q_v.shape[0]
+    n_slots = x_v.shape[0]
+    depth = x_v.shape[1]
+    piece = depth // 4
+
+    q_copy = pltpu.make_async_copy(q_hbm, q_v, local_sem.at[0])
+    q_copy.start()
+
+    def x_copy(c):
+        cols = pl.ds(c * piece, piece)
+        return pltpu.make_async_copy(x_hbm.at[:, cols], x_v.at[:, cols], local_sem.at[1 + c])
+
+    def w_copies(h, t, c):
+        owner = core if t == 0 else sibling
+        head = pl.ds(pl.multiple_of((owner * 2 + h) * HEAD_SIZE, HEAD_SIZE), HEAD_SIZE)
+        rows = pl.ds(c * piece, piece)
+        slot = h * 2 + t
+        return [
+            pltpu.make_async_copy(
+                src.at[rows, head],
+                w_v.at[slot, rows, pl.ds(i * HEAD_SIZE, HEAD_SIZE)],
+                w_sem.at[slot, c, i],
+            )
+            for i, src in enumerate((wk_hbm, wv_hbm))
+        ]
+
+    for c in range(4):
+        x_copy(c).start()
+        for copy in w_copies(0, 1, c):
+            copy.start()
+    for h, t in ((0, 0), (1, 1), (1, 0)):
+        for c in range(4):
+            for copy in w_copies(h, t, c):
+                copy.start()
+
+    def z_to(step):
+        return (z + step) % PLANES
+
+    def plane_to(step):
+        return ((px + step // 4) % 4) * 4 + (py + step % 4) % 4
+
+    def plane_from(step):
+        return ((px + 4 - step // 4) % 4) * 4 + (py + 4 - step % 4) % 4
+
+    barrier = pltpu.get_barrier_semaphore()
+    pl.semaphore_signal(barrier, inc=1, device_id=(doc, sibling), device_id_type=MESH)
+
+    def greet_z(i, carry):
+        pl.semaphore_signal(barrier, inc=1, device_id=(z_to(i) * PLANE + p, core), device_id_type=MESH)
+        return carry
+
+    def greet_plane(i, carry):
+        pl.semaphore_signal(barrier, inc=1, device_id=(z * PLANE + plane_to(i), core), device_id_type=MESH)
+        return carry
+
+    lax.fori_loop(1, PLANES, greet_z, 0)
+    lax.fori_loop(1, PLANE, greet_plane, 0)
+
+    slots_t = slot_ref[...]
+    present = slots_t >= 0
+    there = flag(present)
+    d_row, d_col = iota((128, 128), 0), iota((128, 128), 1)
+    same = (d_row // PLANE) == (d_col // PLANE)
+    before = mm(there, flag(same & (d_row < d_col)))
+    totals = mm(there, flag(same)).astype(jnp.bfloat16)
+    earlier = mm(flag(iota((8, 8), 1) < iota((8, 8), 0)), totals)
+    rank = before + earlier
+    identity = flag(d_row == d_col)
+    slot_cols = mm(identity, slots_t.astype(jnp.float32).astype(jnp.bfloat16), RIGHT)
+    rank_cols = mm(identity, jnp.where(present, rank, 0.0).astype(jnp.bfloat16), RIGHT)
+    plane_base = (CAPACITY * (iota((128, 1), 0) // PLANE)).astype(jnp.float32) + 1.0
+    slot_lane = iota((1, n_slots), 1).astype(jnp.float32)
+    found = jnp.zeros((128, n_slots), jnp.float32)
+    for j in range(IMG_MAX):
+        found = found + jnp.where(
+            slot_cols[:, j : j + 1] == slot_lane, rank_cols[:, j : j + 1] + plane_base, 0.0
+        )
+    goes_to = jnp.sum(found, axis=0, keepdims=True) - 1.0
+    pick1[...] = flag(iota((PLANES * CAPACITY, n_slots), 0).astype(jnp.float32) == goes_to)
+
+    rows_e, cols_e = 4 * PLANE * IMG_MAX, 4 * CAPACITY
+    mine_doc = flag(iota((rows_e, 128), 1) == z * PLANE + iota((rows_e, 128), 0) // (4 * IMG_MAX))
+    rank_plus = jnp.where(present, rank + 1.0, 0.0).astype(jnp.bfloat16)
+    by_slot = mm(mine_doc, rank_plus, RIGHT)
+    chosen = iota((rows_e, IMG_MAX), 1) == iota((rows_e, IMG_MAX), 0) % IMG_MAX
+    row_rank = jnp.sum(jnp.where(chosen, by_slot, 0.0), axis=1, keepdims=True)
+    source = (iota((rows_e, 1), 0) // IMG_MAX) % 4
+    row_target = jnp.where(row_rank > 0.0, row_rank - 1.0 + (CAPACITY * source).astype(jnp.float32), -1.0)
+    expand[...] = flag(iota((rows_e, cols_e), 1).astype(jnp.float32) == row_target)
+
+    lane = iota((1, HEAD_SIZE), 1)
+    first_t = jnp.zeros((1, HEAD_SIZE), jnp.int32)
+    last_t = jnp.zeros((1, HEAD_SIZE), jnp.int32)
+    for j in range(IMG_MAX):
+        first_t = jnp.where(lane == j, pos_ref[0, j], first_t)
+        last_t = jnp.where(lane == j, end_ref[0, j], last_t)
+    block = iota((2 * tokens, HEAD_SIZE), 0) // tokens
+    owner = jnp.where(block == 0, core, sibling)
+    t_pos = owner * tokens + iota((2 * tokens, HEAD_SIZE), 0) % tokens
+    attends = (lane < count_ref[0]) & (first_t <= t_pos) & (t_pos < last_t)
+    q_tail = flag(jnp.logical_not(attends))
+    n_keys = k_tail.shape[0]
+    k_tail[...] = jnp.where(
+        iota((n_keys, HEAD_SIZE), 1) == iota((n_keys, HEAD_SIZE), 0) % IMG_MAX, MASKED, 0.0
+    ).astype(jnp.bfloat16)
+
+    q_copy.wait()
+    q_gain = qg_ref[...]
+    half_width = QUERY_HEADS // 2 * HEAD_SIZE
+
+    def norm_queries(i, carry):
+        at = pl.multiple_of(i * HEAD_SIZE, HEAD_SIZE)
+        own_cols = pl.ds(pl.multiple_of(core * half_width + at, HEAD_SIZE), HEAD_SIZE)
+        sib_cols = pl.ds(pl.multiple_of(sibling * half_width + at, HEAD_SIZE), HEAD_SIZE)
+        q_all[0, :, pl.ds(at, HEAD_SIZE)] = head_norm(q_v[:, own_cols].astype(jnp.float32), q_gain).astype(jnp.bfloat16)
+        q_send[:, pl.ds(at, HEAD_SIZE)] = head_norm(q_v[:, sib_cols].astype(jnp.float32), q_gain).astype(jnp.bfloat16)
+        return carry
+
+    lax.fori_loop(0, QUERY_HEADS // 2, norm_queries, 0)
+
+    def project(h, t):
+        total = None
+        for c in range(4):
+            if (h, t) == (0, 1):
+                x_copy(c).wait()
+            for copy in w_copies(h, t, c):
+                copy.wait()
+            rows = pl.ds(c * piece, piece)
+            term = mm(x_v[:, rows], w_v[h * 2 + t, rows, :])
+            total = term if total is None else total + term
+        return total
+
+    def part_copy(h):
+        return pltpu.make_async_remote_copy(
+            src_ref=part_send.at[h],
+            dst_ref=part_recv.at[h],
+            send_sem=part_sems.at[0, h],
+            recv_sem=part_sems.at[1, h],
+            device_id=(doc, sibling),
+            device_id_type=MESH,
+        )
+
+    q_exchange = pltpu.make_async_remote_copy(
+        src_ref=q_send,
+        dst_ref=q_all.at[1],
+        send_sem=q_sems.at[0],
+        recv_sem=q_sems.at[1],
+        device_id=(doc, sibling),
+        device_id_type=MESH,
+    )
+
+    def hop1(h, i):
+        return pltpu.make_async_remote_copy(
+            src_ref=send1.at[h, z_to(i)],
+            dst_ref=recv1.at[h, z],
+            send_sem=s1_sem.at[h, i - 1],
+            recv_sem=r1_sem.at[h, i - 1],
+            device_id=(z_to(i) * PLANE + p, core),
+            device_id_type=MESH,
+        )
+
+    def hop1_in(h, i):
+        source = z_to(PLANES - i)
+        return pltpu.make_async_remote_copy(
+            src_ref=send1.at[h, source],
+            dst_ref=recv1.at[h, source],
+            send_sem=s1_sem.at[h, i - 1],
+            recv_sem=r1_sem.at[h, i - 1],
+            device_id=(source * PLANE + p, core),
+            device_id_type=MESH,
+        )
+
+    def hop2(h, i):
+        return pltpu.make_async_remote_copy(
+            src_ref=send2.at[h, plane_to(i)],
+            dst_ref=recv2.at[h, p],
+            send_sem=s2_sem.at[h, i - 1],
+            recv_sem=r2_sem.at[h, i - 1],
+            device_id=(z * PLANE + plane_to(i), core),
+            device_id_type=MESH,
+        )
+
+    def hop2_in(h, i):
+        source = plane_from(i)
+        return pltpu.make_async_remote_copy(
+            src_ref=send2.at[h, source],
+            dst_ref=recv2.at[h, source],
+            send_sem=s2_sem.at[h, i - 1],
+            recv_sem=r2_sem.at[h, i - 1],
+            device_id=(z * PLANE + source, core),
+            device_id_type=MESH,
+        )
+
+    def each(low, high, act):
+        def body(i, carry):
+            act(i)
+            return carry
+
+        lax.fori_loop(low, high, body, 0)
+
+    key_gain = kg_ref[...]
+
+    def encode_and_pack(h):
+        part_copy(h).wait_recv()
+        total = part_mine[...] + part_recv[h]
+        keys = head_norm(total[:, :HEAD_SIZE], key_gain).astype(jnp.bfloat16)
+        values = total[:, HEAD_SIZE:].astype(jnp.bfloat16)
+        kv = jnp.concatenate([keys, values], axis=1)
+        packed = mm(pick1[...], kv).astype(jnp.bfloat16)
+        send1[h] = packed.reshape(PLANES, CAPACITY, 2 * HEAD_SIZE)
+        each(1, PLANES, lambda i: hop1(h, i).start())
+        recv1[h, z] = send1[h, z]
+
+    part_send[0] = project(0, 1)
+    pl.semaphore_wait(barrier, PLANES - 1 + PLANE - 1 + 1)
+    part_copy(0).start()
+    part_mine[...] = project(0, 0)
+    part_send[1] = project(1, 1)
+    part_copy(1).start()
+    encode_and_pack(0)
+    q_exchange.start()
+    part_mine[...] = project(1, 0)
+    encode_and_pack(1)
+
+    def expand_and_send(h):
+        each(1, PLANES, lambda i: hop1_in(h, i).wait_recv())
+        for s in range(2):
+            packed = recv1[h, pl.ds(4 * s, 4)].reshape(4 * CAPACITY, 2 * HEAD_SIZE)
+            rows = mm(expand[...], packed).astype(jnp.bfloat16)
+            send2[h, :, pl.ds(4 * IMG_MAX * s, 4 * IMG_MAX), :] = rows.reshape(PLANE, 4 * IMG_MAX, 2 * HEAD_SIZE)
+        each(1, PLANE, lambda i: hop2(h, i).start())
+        recv2[h, p] = send2[h, p]
+
+    expand_and_send(0)
+    expand_and_send(1)
+    q_exchange.wait_recv()
+
+    ones = jnp.ones((n_keys, HEAD_SIZE), jnp.bfloat16)
+    scale = 1.0 / math.sqrt(HEAD_SIZE)
+
+    def o_copy(h):
+        return pltpu.make_async_remote_copy(
+            src_ref=o_send.at[h],
+            dst_ref=o_v.at[core * 2 + h],
+            send_sem=o_sems.at[0, h],
+            recv_sem=o_sems.at[1, h],
+            device_id=(doc, sibling),
+            device_id_type=MESH,
+        )
+
+    def o_in(h):
+        return pltpu.make_async_remote_copy(
+            src_ref=o_send.at[h],
+            dst_ref=o_v.at[sibling * 2 + h],
+            send_sem=o_sems.at[0, h],
+            recv_sem=o_sems.at[1, h],
+            device_id=(doc, sibling),
+            device_id_type=MESH,
+        )
+
+    def out_copy(head, i):
+        return pltpu.make_async_copy(o_v.at[head], out_hbm.at[head], out_sem.at[i])
+
+    def attend(h):
+        each(1, PLANE, lambda i: hop2_in(h, i).wait_recv())
+        kv = recv2[h].reshape(n_keys, 2 * HEAD_SIZE)
+        keys = jnp.concatenate([kv[:, :HEAD_SIZE], k_tail[...]], axis=1)
+        values = jnp.concatenate([kv[:, HEAD_SIZE:], ones], axis=1)
+
+        def head(g, carry):
+            at = pl.multiple_of((h * GROUP + g) * HEAD_SIZE, HEAD_SIZE)
+            q = q_all[:, :, pl.ds(at, HEAD_SIZE)].reshape(2 * tokens, HEAD_SIZE)
+            scores = mm(jnp.concatenate([q, q_tail], axis=1), keys, RIGHT)
+            weights = jnp.exp(scores * scale).astype(jnp.bfloat16)
+            mixed = mm(weights, values)
+            total = mixed[:, HEAD_SIZE:]
+            out = (mixed[:, :HEAD_SIZE] / jnp.where(total > 0.0, total, 1.0)).astype(jnp.bfloat16)
+            cols = pl.ds(pl.multiple_of(g * HEAD_SIZE, HEAD_SIZE), HEAD_SIZE)
+            o_v[core * 2 + h, :, cols] = out[:tokens]
+            o_send[h, :, cols] = out[tokens:]
+            return carry
+
+        lax.fori_loop(0, GROUP, head, 0)
+        o_copy(h).start()
+        out_copy(core * 2 + h, h).start()
+
+    attend(0)
+    attend(1)
+    for h in range(2):
+        o_in(h).wait_recv()
+        out_copy(sibling * 2 + h, 2 + h).start()
+    for h in range(2):
+        part_copy(h).wait_send()
+        each(1, PLANES, lambda i: hop1(h, i).wait_send())
+        each(1, PLANE, lambda i: hop2(h, i).wait_send())
+        o_copy(h).wait_send()
+    q_exchange.wait_send()
+    for h in range(2):
+        out_copy(core * 2 + h, h).wait()
+        out_copy(sibling * 2 + h, 2 + h).wait()
+
+
+def packed_route(
+    queries,
+    vision,
+    key_matrix,
+    value_matrix,
+    query_gain,
+    key_gain,
+    image_count,
+    image_slot,
+    image_pos,
+    span_end,
+):
+    tokens, width = queries.shape
+    n_slots = vision.shape[0]
+    depth = vision.shape[2]
+    two = 2 * HEAD_SIZE
+    anywhere = pl.BlockSpec(memory_space=pl.ANY)
+    vmem = pl.BlockSpec(memory_space=pltpu.VMEM)
+    smem = pl.BlockSpec(memory_space=pltpu.SMEM)
+    bf16, f32 = jnp.bfloat16, jnp.float32
+    dma = pltpu.SemaphoreType.DMA
+    out = pl.pallas_call(
+        fused_kernel,
+        out_shape=jax.ShapeDtypeStruct((KEY_VALUE_HEADS, tokens, GROUP * HEAD_SIZE), bf16),
+        in_specs=[anywhere, anywhere, anywhere, anywhere, vmem, vmem, smem, vmem, smem, smem],
+        out_specs=anywhere,
+        scratch_shapes=[
+            pltpu.VMEM((tokens, width), bf16),
+            pltpu.VMEM((n_slots, depth), bf16),
+            pltpu.VMEM((4, depth, two), bf16),
+            pltpu.VMEM((2, n_slots, two), f32),
+            pltpu.VMEM((2, n_slots, two), f32),
+            pltpu.VMEM((n_slots, two), f32),
+            pltpu.VMEM((PLANES * CAPACITY, n_slots), bf16),
+            pltpu.VMEM((4 * PLANE * IMG_MAX, 4 * CAPACITY), bf16),
+            pltpu.VMEM((2, PLANES, CAPACITY, two), bf16),
+            pltpu.VMEM((2, PLANES, CAPACITY, two), bf16),
+            pltpu.VMEM((2, PLANE, PLANES * IMG_MAX, two), bf16),
+            pltpu.VMEM((2, PLANE, PLANES * IMG_MAX, two), bf16),
+            pltpu.VMEM((tokens, width // 2), bf16),
+            pltpu.VMEM((2, tokens, width // 2), bf16),
+            pltpu.VMEM((PLANE * PLANES * IMG_MAX, HEAD_SIZE), bf16),
+            pltpu.VMEM((KEY_VALUE_HEADS, tokens, GROUP * HEAD_SIZE), bf16),
+            pltpu.VMEM((2, tokens, GROUP * HEAD_SIZE), bf16),
+            dma((5,)),
+            dma((4, 4, 2)),
+            dma((4,)),
+            dma((2, 2)),
+            dma((2,)),
+            dma((2, 2)),
+            dma((2, PLANES - 1)),
+            dma((2, PLANES - 1)),
+            dma((2, PLANE - 1)),
+            dma((2, PLANE - 1)),
+        ],
+        compiler_params=pltpu.CompilerParams(
+            collective_id=0, has_side_effects=True, vmem_limit_bytes=48 * 1024 * 1024
+        ),
+        name="fused_cross_attention",
+    )(
+        queries,
+        vision.reshape(n_slots, depth),
+        key_matrix,
+        value_matrix,
+        query_gain.reshape(1, HEAD_SIZE),
+        key_gain.reshape(1, HEAD_SIZE),
+        image_count,
+        image_slot.T,
+        image_pos,
+        span_end,
+    )
+    return out.transpose(1, 0, 2).reshape(tokens, width)
+
+
+def shards(*arrays):
+    image_slot = arrays[7]
+    per_plane = jnp.sum((image_slot >= 0).reshape(PLANES, -1).astype(jnp.int32), axis=1)
+    return lax.cond(jnp.max(per_plane) <= CAPACITY, packed_route, general_route, *arrays)
+
+
 def solution(mesh):
     in_specs = (
         P(("doc", "seq"), None),

time: 103 us -> 53.7 us (0.52)
  Pallas kernels: 0 us -> 48.9 us
  waiting for transfers between devices: 26.3 us -> 0 us
  local copies, waits for them, and re-layouts: 25.1 us -> 2.24 us
  starting transfers between devices: 20.2 us -> 0 us
  other arithmetic: 17.7 us -> 1.46 us
  matrix products: 12.2 us -> 0 us
    pallas_call x0 -> x1, Pallas kernels: none -> 48.9 us  [packed_route(): pl.pallas_call(fused_kernel, out_shape=jax.ShapeDtypeStruct((KEY_VALUE_HE...]
    all_to_all x1 -> x0, waiting for transfers between devices: 24.2 us -> none  [shards(): got = lax.all_to_all(packed, 'doc', split_axis=0, concat_axis=0, tiled=True)]
    all_to_all x1 -> x0, starting transfers between devices: 13.8 us -> none  [shards(): got = lax.all_to_all(packed, 'doc', split_axis=0, concat_axis=0, tiled=True)]
    unnamed x30 -> x2, local copies, waits for them, and re-layouts: 13.6 us -> 0.96 us
    dot_general x5 -> x0, matrix products: 12.2 us -> none  [the longest x1 4.64 us: shards(): jnp.einsum('tkgd,nkd->tkgn', q, both[:, 0], preferred_element_type=jnp.fl...]
    all_to_all x1 -> x0, other arithmetic: 8.38 us -> none  [shards(): got = lax.all_to_all(packed, 'doc', split_axis=0, concat_axis=0, tiled=True)]
    ppermute x2 -> x0, starting transfers between devices: 6.39 us -> none  [the longest x1 3.24 us: shards(): mine = pick(core) + lax.ppermute(pick(1 - core), 'seq', other)]
    concatenate x3 -> x0, local copies, waits for them, and re-layouts: 4.61 us -> none  [shards(): both = jnp.concatenate([first, second], axis=3)]
  transfers between devices with their start and end apart: 3 -> 0, of which waited for: 3 -> 0; matrix products, arithmetic and copies ran while one was open for 5% -> 0% of each run, Pallas kernels for 0% -> 0%
where the time goes in v2:
time: 53.7 us; the launch traced here: 53.5 us
  Pallas kernels  48.9 us (91%)
  local copies, waits for them, and re-layouts  2.24 us (4%)
  other arithmetic  1.46 us (3%)
  between operations  0.67 us (1%)
    pallas_call x1, Pallas kernels, packed_route(): pl.pallas_call(fused_kernel, out_shape=jax.ShapeDtypeStruct((KEY_VALUE_HE...  48.9 us

profile of v2, /device:TPU:1, one launch (start us, length us, event | category | flops | bytes accessed | tf_op | source)
XLA Modules:
  0.0 53.5 jit_solution(2078718427807199961)
XLA Ops:
  0.0 0.7 %convert_reduce_fusion.1 = s32[128]{0:T(128)S(1)} fusion(s32[128,8]{0,1:T(8,128)} %param.19), kind=kLoop, calls=%fused_computation.45 | loop fusion | flops 2944 | bytes 4608 | tf_op jit(solution)/shard_map/reduce_sum | solution.py:532
  0.7 0.1 reduce_sum.44
  0.8 0.1 reduce_sum.45
  0.9 0.6 %reduce_max.9 = s32[]{:T(128)} reduce(s32[8]{0:T(128)S(1)} %reduce_sum.45, s32[]{:T(128)} %constant.12.clone.1), dimensions={0}, to_apply=%region_2.3 | reduce | flops 7 | bytes 40 | tf_op jit(solution)/shard_map/reduce_max | solution.py:533
  2.2 50.3 %conditional.1 = (bf16[128,4096]{1,0:T(8,128)(2,1)S(1)}) conditional(s32[]{:T(128)} %convert_element_type.32, (s32[1]{0:T(128)}, s32[1,8]{1,0:T(1,128)}, s32[1,8]{1,0:T(1,128)}, s32[128,8]{0,1:T(8,128)}, bf16[256,1,4096]{2,0,1:T(8,128)(2,1)}, /*index=5*/bf16[4096,512]{1,0:T(8,128)(2,1)}, bf16[4096,512]{1,0:T(8,128)(2,1)}, f32[128]{0:T(128)}, ...), branch_computations={%region_3.8_spmd, %region_8.9_spmd} | conditional | flops 4592182784 | bytes 141282944 | solution.py:533
  2.4 48.9 %fused_cross_attention.1 = bf16[4,128,1024]{2,1,0:T(8,128)(2,1)S(1)} custom-call(bf16[128,4096]{1,0:T(8,128)(2,1)} %get-tuple-element.58.q_hbm, bf16[256,4096]{1,0:T(8,128)(2,1)} %bitcast.70, bf16[4096,512]{1,0:T(8,128)(2,1)} %get-tuple-element.60.wk_hbm, bf16[4096,512]{1,0:T(8,128)(2,1)} %get-tuple-element.61.wv_hbm, f32[1,128]{1,0:T(1,128)} %bitcast.76, ...), custom_call_target="tpu_custom_call" | custom-call | tf_op jit(solution)/shard_map/cond/branch_1_fun/fused_cross_attention/pallas_call | solution.py:477
  51.3 0.7 %copy.73 = bf16[128,4,1024]{0,2,1:T(8,128)(2,1)S(1)} copy(bf16[128,4,1024]{2,0,1:T(8,128)(2,1)S(1)} %bitcast.66) | data formatting | bytes 2097152 | tf_op jit(solution)/shard_map/cond/branch_1_fun/transpose | solution.py:527
  52.0 0.5 copy.82
  52.5 0.0 copy-start.6
  52.5 1.0 %copy-done.6 = bf16[128,4096]{1,0:T(8,128)(2,1)} copy-done((bf16[128,4096]{1,0:T(8,128)(2,1)}, bf16[128,4096]{1,0:T(8,128)(2,1)S(1)}, u32[]{:S(2)}) %copy-start.6) | copy-done | bytes 1048600
Async XLA Ops:
  52.5 1.0 %copy-start.6 = (bf16[128,4096]{1,0:T(8,128)(2,1)}, bf16[128,4096]{1,0:T(8,128)(2,1)S(1)}, u32[]{:S(2)}) copy-start(bf16[128,4096]{1,0:T(8,128)(2,1)S(1)} %get-tuple-element.145) | copy-start | bytes 3145732

commit v3 on v2

v3 whole, which is shorter than its diff:
```python
import functools
import math

import jax
import jax.numpy as jnp
from jax import lax
from jax.experimental import pallas as pl
from jax.experimental.pallas import tpu as pltpu
from jax.sharding import PartitionSpec as P

HEAD_SIZE = 128
QUERY_HEADS = 32
KEY_VALUE_HEADS = 4
IMG_MAX = 8
GROUP = QUERY_HEADS // KEY_VALUE_HEADS
PLANE = 16
PLANES = 8
CAPACITY = 48
MESH = pl.DeviceIdType.MESH
MASKED = -32768.0
PIECES = 8
UNROLL = 4
Z_STEPS = (0, 1, 7, 2, 6, 3, 5, 4)

epsilon = 1e-05


def head_norm(values, scales):
    mean_square = jnp.mean(values * values, axis=-1, keepdims=True)
    return values * lax.rsqrt(mean_square + epsilon) * scales


def general_route(
    queries,
    vision,
    key_matrix,
    value_matrix,
    query_gain,
    key_gain,
    image_count,
    image_slot,
    image_pos,
    span_end,
):
    n_slots = vision.shape[0]
    core = lax.axis_index("seq")
    rows = vision.reshape(n_slots, -1)
    keys = jnp.dot(rows, key_matrix, preferred_element_type=jnp.float32)
    values = jnp.dot(rows, value_matrix, preferred_element_type=jnp.float32)
    half = keys.shape[1] // 2
    other = [(0, 1), (1, 0)]

    def pick(c):
        start = c * half
        return jnp.concatenate(
            [lax.dynamic_slice_in_dim(keys, start, half, 1), lax.dynamic_slice_in_dim(values, start, half, 1)], axis=1
        )

    mine = pick(core) + lax.ppermute(pick(1 - core), "seq", other)
    mine = mine.reshape(n_slots, 2, 2, HEAD_SIZE)
    kv = jnp.concatenate(
        [head_norm(mine[:, 0], key_gain).astype(jnp.bfloat16), mine[:, 1].astype(jnp.bfloat16)], axis=1
    ).reshape(n_slots, 4 * HEAD_SIZE)
    slots = image_slot.reshape(-1)
    one_hot = (slots[:, None] == jnp.arange(n_slots, dtype=jnp.int32)[None, :]).astype(jnp.bfloat16)
    packed = jnp.dot(one_hot, kv, preferred_element_type=jnp.float32).astype(jnp.bfloat16)
    packed = packed.reshape(image_slot.shape[0], IMG_MAX * 4 * HEAD_SIZE)
    got = lax.all_to_all(packed, "doc", split_axis=0, concat_axis=0, tiled=True)
    theirs = lax.ppermute(got, "seq", other)
    first = jnp.where(core == 0, got, theirs).reshape(-1, IMG_MAX, 2, 2, HEAD_SIZE)
    second = jnp.where(core == 0, theirs, got).reshape(-1, IMG_MAX, 2, 2, HEAD_SIZE)
    both = jnp.concatenate([first, second], axis=3)
    n_keys = both.shape[0] * IMG_MAX
    both = both.reshape(n_keys, 2, KEY_VALUE_HEADS, HEAD_SIZE)
    local_tokens = queries.shape[0]
    positions = core * local_tokens + jnp.arange(local_tokens, dtype=jnp.int32)
    q = queries.astype(jnp.float32).reshape(local_tokens, KEY_VALUE_HEADS, GROUP, HEAD_SIZE)
    q = head_norm(q, query_gain).astype(jnp.bfloat16)
    seen = jnp.arange(IMG_MAX, dtype=jnp.int32)
    attends = (
        (seen[None, :] < image_count[0])
        & (image_pos[0][None, :] <= positions[:, None])
        & (positions[:, None] < span_end[0][None, :])
    )
    scores = jnp.einsum("tkgd,nkd->tkgn", q, both[:, 0], preferred_element_type=jnp.float32)
    scores = scores * (1.0 / math.sqrt(HEAD_SIZE))
    key_mask = jnp.tile(attends, (1, n_keys // IMG_MAX))
    weights = jnp.where(key_mask[:, None, None, :], jnp.exp(scores), 0.0).astype(jnp.bfloat16)
    numerator = jnp.einsum("tkgn,nkd->tkgd", weights, both[:, 1], preferred_element_type=jnp.float32)
    denominator = jnp.sum(weights, axis=3, dtype=jnp.float32)
    reached = jnp.any(attends, axis=1)[:, None, None]
    quotient = numerator / jnp.where(reached, denominator, 1.0)[..., None]
    mixed_rows = jnp.where(reached[..., None], quotient, 0.0).astype(jnp.bfloat16)
    return mixed_rows.reshape(local_tokens, QUERY_HEADS * HEAD_SIZE)


def iota(shape, axis):
    return lax.broadcasted_iota(jnp.int32, shape, axis)


def flag(condition):
    return condition.astype(jnp.float32).astype(jnp.bfloat16)


def mm(a, b, contract=((1,), (0,))):
    return lax.dot_general(a, b, (contract, ((), ())), preferred_element_type=jnp.float32)


RIGHT = ((1,), (1,))


def fused_kernel(
    q_hbm,
    x_hbm,
    wk_hbm,
    wv_hbm,
    qg_ref,
    kg_ref,
    count_ref,
    slot_ref,
    pos_ref,
    end_ref,
    out_hbm,
    q_v,
    x_v,
    wk_v,
    wv_v,
    sum_k,
    sum_v,
    got_k,
    got_v,
    pick1,
    expand,
    send1,
    recv1,
    send2,
    recv2,
    q_send,
    q_all,
    q_tail,
    k_tail,
    o_sum,
    o_own,
    o_send,
    local_sem,
    w_sem,
    out_sem,
    part_sems,
    q_sems,
    o_sems,
    s1_sem,
    r1_sem,
    s2_sem,
    r2_sem,
):
    doc = lax.axis_index("doc")
    core = lax.axis_index("seq")
    sibling = 1 - core
    z, p = doc // PLANE, doc % PLANE
    px, py = p // 4, p % 4
    tokens = q_v.shape[0]
    n_slots, depth = x_v.shape
    piece = depth // PIECES
    row_block = n_slots // 4
    half = KEY_VALUE_HEADS // 2 * HEAD_SIZE
    own_half = pl.ds(pl.multiple_of(core * half, half), half)
    sib_half = pl.ds(pl.multiple_of(sibling * half, half), half)

    def x_copy(i):
        rows = pl.ds(i * row_block, row_block)
        return pltpu.make_async_copy(x_hbm.at[rows], x_v.at[rows], local_sem.at[i])

    q_copy = pltpu.make_async_copy(q_hbm, q_v, local_sem.at[4])

    def w_copy(i, c):
        rows = pl.ds(c * piece, piece)
        hbm, v = ((wk_hbm, wk_v), (wv_hbm, wv_v))[i]
        return pltpu.make_async_copy(hbm.at[rows], v.at[rows], w_sem.at[i, c])

    for i in range(4):
        x_copy(i).start()
    for c in range(PIECES):
        w_copy(0, c).start()
        w_copy(1, c).start()
    q_copy.start()

    def z_to(s):
        return (z + Z_STEPS[s]) % PLANES

    def plane_to(i):
        return ((px + i // 4) % 4) * 4 + (py + i % 4) % 4

    barrier = pltpu.get_barrier_semaphore()
    pl.semaphore_signal(barrier, inc=1, device_id=(doc, sibling), device_id_type=MESH)

    def greet_z(i, carry):
        there = ((z + i) % PLANES) * PLANE + p
        pl.semaphore_signal(barrier, inc=1, device_id=(there, core), device_id_type=MESH)
        return carry

    def greet_plane(i, carry):
        pl.semaphore_signal(barrier, inc=1, device_id=(z * PLANE + plane_to(i), core), device_id_type=MESH)
        return carry

    lax.fori_loop(1, PLANES, greet_z, 0)
    lax.fori_loop(1, PLANE, greet_plane, 0)

    slots_t = slot_ref[...]
    present = slots_t >= 0
    there = flag(present)
    d_row, d_col = iota((128, 128), 0), iota((128, 128), 1)
    same = (d_row // PLANE) == (d_col // PLANE)
    before = mm(there, flag(same & (d_row < d_col)))
    totals = mm(there, flag(same)).astype(jnp.bfloat16)
    earlier = mm(flag(iota((8, 8), 1) < iota((8, 8), 0)), totals)
    rank = before + earlier
    identity = flag(d_row == d_col)
    slot_cols = mm(identity, slots_t.astype(jnp.float32).astype(jnp.bfloat16), RIGHT)
    rank_cols = mm(identity, jnp.where(present, rank, 0.0).astype(jnp.bfloat16), RIGHT)
    away = (iota((128, 1), 0) // PLANE + PLANES - z) % PLANES
    z_slot = jnp.where(away == 0, 0, jnp.where(away <= PLANES // 2, 2 * away - 1, 2 * (PLANES - away)))
    plane_base = (CAPACITY * z_slot).astype(jnp.float32) + 1.0
    slot_lane = iota((1, n_slots), 1).astype(jnp.float32)
    found = jnp.zeros((128, n_slots), jnp.float32)
    for j in range(IMG_MAX):
        found = found + jnp.where(
            slot_cols[:, j : j + 1] == slot_lane, rank_cols[:, j : j + 1] + plane_base, 0.0
        )
    goes_to = jnp.sum(found, axis=0, keepdims=True) - 1.0
    pick1[...] = flag(iota((PLANES * CAPACITY, n_slots), 0).astype(jnp.float32) == goes_to)

    pair = 2 * IMG_MAX
    rows_e, cols_e = PLANE * pair, 2 * CAPACITY
    row_step = iota((rows_e, 128), 0) // pair
    row_doc = z * PLANE + ((px + row_step // 4) % 4) * 4 + (py + row_step % 4) % 4
    mine_doc = flag(iota((rows_e, 128), 1) == row_doc)
    rank_plus = jnp.where(present, rank + 1.0, 0.0).astype(jnp.bfloat16)
    by_slot = mm(mine_doc, rank_plus, RIGHT)
    chosen = iota((rows_e, IMG_MAX), 1) == iota((rows_e, IMG_MAX), 0) % IMG_MAX
    row_rank = jnp.sum(jnp.where(chosen, by_slot, 0.0), axis=1, keepdims=True)
    source = (iota((rows_e, 1), 0) // IMG_MAX) % 2
    row_target = jnp.where(row_rank > 0.0, row_rank - 1.0 + (CAPACITY * source).astype(jnp.float32), -1.0)
    expand[...] = flag(iota((rows_e, cols_e), 1).astype(jnp.float32) == row_target)

    lane = iota((1, HEAD_SIZE), 1)
    first_t = jnp.zeros((1, HEAD_SIZE), jnp.int32)
    last_t = jnp.zeros((1, HEAD_SIZE), jnp.int32)
    for j in range(IMG_MAX):
        first_t = jnp.where(lane == j, pos_ref[0, j], first_t)
        last_t = jnp.where(lane == j, end_ref[0, j], last_t)
    block = iota((2 * tokens, HEAD_SIZE), 0) // tokens
    owner = jnp.where(block == 0, core, sibling)
    t_pos = owner * tokens + iota((2 * tokens, HEAD_SIZE), 0) % tokens
    attends = (lane < count_ref[0]) & (first_t <= t_pos) & (t_pos < last_t)
    q_tail[...] = flag(jnp.logical_not(attends))
    n_keys = k_tail.shape[0]
    k_tail[...] = jnp.where(
        iota((n_keys, HEAD_SIZE), 1) == iota((n_keys, HEAD_SIZE), 0) % IMG_MAX, MASKED, 0.0
    ).astype(jnp.bfloat16)

    for i in range(4):
        x_copy(i).wait()
    for c in range(PIECES):
        cols = pl.ds(c * piece, piece)
        for i, (w, total) in enumerate(((wk_v, sum_k), (wv_v, sum_v))):
            w_copy(i, c).wait()
            term = mm(x_v[:, cols], w[cols, :])
            total[...] = term if c == 0 else total[...] + term

    def part_copy(i):
        total, got = ((sum_k, got_k), (sum_v, got_v))[i]
        return pltpu.make_async_remote_copy(
            src_ref=total.at[:, sib_half],
            dst_ref=got,
            send_sem=part_sems.at[0, i],
            recv_sem=part_sems.at[1, i],
            device_id=(doc, sibling),
            device_id_type=MESH,
        )

    pl.semaphore_wait(barrier, PLANES - 1 + PLANE - 1 + 1)
    part_copy(0).start()
    part_copy(1).start()

    q_copy.wait()
    q_gain = qg_ref[...]
    half_width = QUERY_HEADS // 2 * HEAD_SIZE

    def norm_queries(i, carry):
        at = pl.multiple_of(i * HEAD_SIZE, HEAD_SIZE)
        own_cols = pl.ds(pl.multiple_of(core * half_width + at, HEAD_SIZE), HEAD_SIZE)
        sib_cols = pl.ds(pl.multiple_of(sibling * half_width + at, HEAD_SIZE), HEAD_SIZE)
        q_all[0, :, pl.ds(at, HEAD_SIZE)] = head_norm(q_v[:, own_cols].astype(jnp.float32), q_gain).astype(jnp.bfloat16)
        q_send[:, pl.ds(at, HEAD_SIZE)] = head_norm(q_v[:, sib_cols].astype(jnp.float32), q_gain).astype(jnp.bfloat16)
        return carry

    def norm_all_queries():
        lax.fori_loop(0, QUERY_HEADS // 2, norm_queries, 0)

    q_exchange = pltpu.make_async_remote_copy(
        src_ref=q_send,
        dst_ref=q_all.at[1],
        send_sem=q_sems.at[0],
        recv_sem=q_sems.at[1],
        device_id=(doc, sibling),
        device_id_type=MESH,
    )

    def hop1(s):
        return pltpu.make_async_remote_copy(
            src_ref=send1.at[s],
            dst_ref=recv1.at[s],
            send_sem=s1_sem.at[s],
            recv_sem=r1_sem.at[s],
            device_id=(z_to(s) * PLANE + p, core),
            device_id_type=MESH,
        )

    def hop2(k, i):
        return pltpu.make_async_remote_copy(
            src_ref=send2.at[k, i],
            dst_ref=recv2.at[k, i],
            send_sem=s2_sem.at[k],
            recv_sem=r2_sem.at[k],
            device_id=(z * PLANE + plane_to(i), core),
            device_id_type=MESH,
        )

    def await_group(ref, k, sem):
        part = ref.at[k, pl.ds(1, PLANE - 1)]
        pltpu.make_async_copy(part, part, sem.at[k]).wait()

    key_gain = kg_ref[...]
    part_copy(0).wait_recv()
    raw_k = sum_k[:, own_half] + got_k[...]
    keys_own = [head_norm(raw_k[:, h * HEAD_SIZE : (h + 1) * HEAD_SIZE], key_gain).astype(jnp.bfloat16) for h in range(2)]
    part_copy(1).wait_recv()
    raw_v = (sum_v[:, own_half] + got_v[...]).astype(jnp.bfloat16)
    kv_own = jnp.concatenate(keys_own + [raw_v], axis=1)
    packed = mm(pick1[...], kv_own).astype(jnp.bfloat16).reshape(PLANES, CAPACITY, 2 * half)
    recv1[0] = packed[0]
    for s in range(1, PLANES):
        send1[s] = packed[s]
    for s in range(1, PLANES):
        hop1(s).start()
    norm_all_queries()
    q_exchange.start()

    def expand_and_send(k):
        for s in (2 * k, 2 * k + 1):
            if s > 0:
                hop1(s).wait_recv()
        rows = mm(expand[...], recv1[pl.ds(2 * k, 2)].reshape(2 * CAPACITY, 2 * half)).astype(jnp.bfloat16)
        rows = rows.reshape(PLANE, pair, 2 * half)
        recv2[k, 0] = rows[0]
        send2[k, pl.ds(1, PLANE - 1)] = rows[1:]

        def body(i, carry):
            hop2(k, i).start()
            return carry

        lax.fori_loop(1, PLANE, body, 0)

    ones = jnp.ones((n_keys, HEAD_SIZE), jnp.bfloat16)
    scale = 1.0 / math.sqrt(HEAD_SIZE)
    last = PLANES // 2 - 1

    def attend(k):
        await_group(recv2, k, r2_sem)

        def heads(n, carry):
            h = n // (GROUP // UNROLL)
            k_cols = pl.ds(pl.multiple_of(h * HEAD_SIZE, HEAD_SIZE), HEAD_SIZE)
            v_cols = pl.ds(pl.multiple_of(half + h * HEAD_SIZE, HEAD_SIZE), HEAD_SIZE)
            keys = jnp.concatenate([recv2[k, :, :, k_cols].reshape(n_keys, HEAD_SIZE), k_tail[...]], axis=1)
            values = jnp.concatenate([recv2[k, :, :, v_cols].reshape(n_keys, HEAD_SIZE), ones], axis=1)
            for u in range(UNROLL):
                g = n * UNROLL + u
                cols = pl.ds(pl.multiple_of(g * HEAD_SIZE, HEAD_SIZE), HEAD_SIZE)
                q = q_all[:, :, cols].reshape(2 * tokens, HEAD_SIZE)
                scores = mm(jnp.concatenate([q, q_tail[...]], axis=1), keys, RIGHT)
                weights = jnp.exp(scores * scale).astype(jnp.bfloat16)
                mixed = mm(weights, values)
                if k > 0:
                    mixed = mixed + o_sum[g]
                if k < last:
                    o_sum[g] = mixed
                else:
                    total = mixed[:, HEAD_SIZE:]
                    out = (mixed[:, :HEAD_SIZE] / jnp.where(total > 0.0, total, 1.0)).astype(jnp.bfloat16)
                    o_own[:, cols] = out[:tokens]
                    o_send[:, cols] = out[tokens:]
            return carry

        per_head = GROUP // UNROLL
        if k < last:
            lax.fori_loop(0, 2 * per_head, heads, 0)
        else:
            for h in range(2):
                lax.fori_loop(h * per_head, (h + 1) * per_head, heads, 0)
                o_copy(h).start()
                own_copy(h).start()

    out_width = GROUP * HEAD_SIZE

    def out_at(of, h):
        return out_hbm.at[:, pl.ds(pl.multiple_of((of * 2 + h) * out_width, out_width), out_width)]

    def o_copy(h):
        return pltpu.make_async_remote_copy(
            src_ref=o_send.at[:, pl.ds(h * out_width, out_width)],
            dst_ref=out_at(core, h),
            send_sem=o_sems.at[0, h],
            recv_sem=o_sems.at[1, h],
            device_id=(doc, sibling),
            device_id_type=MESH,
        )

    def o_in(h):
        return pltpu.make_async_remote_copy(
            src_ref=o_send.at[:, pl.ds(h * out_width, out_width)],
            dst_ref=out_at(sibling, h),
            send_sem=o_sems.at[0, h],
            recv_sem=o_sems.at[1, h],
            device_id=(doc, sibling),
            device_id_type=MESH,
        )

    def own_copy(h):
        return pltpu.make_async_copy(o_own.at[:, pl.ds(h * out_width, out_width)], out_at(core, h), out_sem.at[h])

    expand_and_send(0)
    expand_and_send(1)
    expand_and_send(2)
    q_exchange.wait_recv()
    attend(0)
    expand_and_send(3)
    attend(1)
    attend(2)
    attend(3)

    for i in range(2):
        part_copy(i).wait_send()
    for s in range(1, PLANES):
        hop1(s).wait_send()
    for k in range(last + 1):
        await_group(send2, k, s2_sem)
    q_exchange.wait_send()
    for h in range(2):
        o_copy(h).wait_send()
        own_copy(h).wait()
        o_in(h).wait_recv()


def packed_route(
    queries,
    vision,
    key_matrix,
    value_matrix,
    query_gain,
    key_gain,
    image_count,
    image_slot,
    image_pos,
    span_end,
):
    tokens, width = queries.shape
    n_slots = vision.shape[0]
    depth = vision.shape[2]
    two = 2 * HEAD_SIZE
    anywhere = pl.BlockSpec(memory_space=pl.ANY)
    vmem = pl.BlockSpec(memory_space=pltpu.VMEM)
    smem = pl.BlockSpec(memory_space=pltpu.SMEM)
    bf16, f32 = jnp.bfloat16, jnp.float32
    dma = pltpu.SemaphoreType.DMA
    groups = PLANES // 2
    pair = 2 * IMG_MAX
    out = pl.pallas_call(
        fused_kernel,
        out_shape=jax.ShapeDtypeStruct((tokens, width), bf16),
        in_specs=[anywhere, anywhere, anywhere, anywhere, vmem, vmem, smem, vmem, smem, smem],
        out_specs=anywhere,
        scratch_shapes=[
            pltpu.VMEM((tokens, width), bf16),
            pltpu.VMEM((n_slots, depth), bf16),
            pltpu.VMEM(key_matrix.shape, bf16),
            pltpu.VMEM(value_matrix.shape, bf16),
            pltpu.VMEM((n_slots, 2 * two), f32),
            pltpu.VMEM((n_slots, 2 * two), f32),
            pltpu.VMEM((n_slots, two), f32),
            pltpu.VMEM((n_slots, two), f32),
            pltpu.VMEM((PLANES * CAPACITY, n_slots), bf16),
            pltpu.VMEM((PLANE * pair, 2 * CAPACITY), bf16),
            pltpu.VMEM((PLANES, CAPACITY, 2 * two), bf16),
            pltpu.VMEM((PLANES, CAPACITY, 2 * two), bf16),
            pltpu.VMEM((groups, PLANE, pair, 2 * two), bf16),
            pltpu.VMEM((groups, PLANE, pair, 2 * two), bf16),
            pltpu.VMEM((tokens, width // 2), bf16),
            pltpu.VMEM((2, tokens, width // 2), bf16),
            pltpu.VMEM((2 * tokens, HEAD_SIZE), bf16),
            pltpu.VMEM((PLANE * pair, HEAD_SIZE), bf16),
            pltpu.VMEM((2 * GROUP, 2 * tokens, two), f32),
            pltpu.VMEM((tokens, width // 2), bf16),
            pltpu.VMEM((tokens, width // 2), bf16),
            dma((5,)),
            dma((2, PIECES)),
            dma((2,)),
            dma((2, 2)),
            dma((2,)),
            dma((2, 2)),
            dma((PLANES,)),
            dma((PLANES,)),
            dma((groups,)),
            dma((groups,)),
        ],
        compiler_params=pltpu.CompilerParams(
            collective_id=0, has_side_effects=True, vmem_limit_bytes=56 * 1024 * 1024
        ),
        name="fused_cross_attention",
    )(
        queries,
        vision.reshape(n_slots, depth),
        key_matrix,
        value_matrix,
        query_gain.reshape(1, HEAD_SIZE),
        key_gain.reshape(1, HEAD_SIZE),
        image_count,
        image_slot.T,
        image_pos,
        span_end,
    )
    return out


def shards(*arrays):
    image_slot = arrays[7]
    shift = 8 * (jnp.arange(image_slot.shape[0], dtype=jnp.uint32) // PLANE % 4)
    part = jnp.where(image_slot >= 0, jnp.uint32(1) << shift[:, None], jnp.uint32(0))
    words = [jnp.sum(part[: 4 * PLANE]), jnp.sum(part[4 * PLANE :])]
    fits = jnp.bool_(True)
    for word in words:
        for i in range(4):
            fits = fits & (((word >> (8 * i)) & 255) <= CAPACITY)
    return lax.cond(fits, packed_route, general_route, *arrays)

def solution(mesh):
    in_specs = (
        P(("doc", "seq"), None),
        P(None, "doc", "seq"),
        P("seq", None),
        P("seq", None),
        P(),
        P(),
        P("doc"),
        P(),
        P("doc", None),
        P("doc", None),
    )
    out_specs = P(("doc", "seq"), None)
    return jax.shard_map(shards, mesh=mesh, in_specs=in_specs, out_specs=out_specs, check_vma=False)
```

time: 53.7 us -> 51.8 us (0.965)
  Pallas kernels: 48.9 us -> 43.8 us
  between operations: 0.67 us -> 5.15 us
  local copies, waits for them, and re-layouts: 2.24 us -> 0.97 us
    pallas_call x1, Pallas kernels: 48.9 us -> 43.8 us  [packed_route(): pl.pallas_call(fused_kernel, out_shape=jax.ShapeDtypeStruct((tokens, widt...]
    select_n x0 -> x1, other arithmetic: none -> 0.69 us  [shards(): jnp.where(image_slot >= 0, jnp.uint32(1) << shift[:, None], jnp.uint32(0))]
    transpose x1 -> x0, local copies, waits for them, and re-layouts: 0.66 us -> none  [packed_route(): return out.transpose(1, 0, 2).reshape(tokens, width)]
    reduce_max x1 -> x0, other arithmetic: 0.64 us -> none  [shards(): jnp.max(per_plane) <= CAPACITY]
where the time goes in v3:
time: 51.8 us; the launch traced here: 51.6 us
  Pallas kernels  43.8 us (85%)
  between operations  5.15 us (10%)
  other arithmetic  1.46 us (3%)
  local copies, waits for them, and re-layouts  0.97 us (2%)
    pallas_call x1, Pallas kernels, packed_route(): pl.pallas_call(fused_kernel, out_shape=jax.ShapeDtypeStruct((tokens, widt...  43.8 us

profile of v3, /device:TPU:1, one launch (start us, length us, event | category | flops | bytes accessed | tf_op | source)
XLA Modules:
  0.0 51.6 jit_solution(891651286917339310)
XLA Ops:
  0.0 0.7 %compare_select_fusion = u32[128,8]{0,1:T(8,128)S(1)} fusion(s32[128,8]{0,1:T(8,128)} %param.19, u32[128]{0:T(128)S(1)} %multiply_shift-left_fusion), kind=kLoop, calls=%fused_computation.47 | loop fusion | flops 2048 | bytes 8704 | tf_op jit(solution)/shard_map/jit(_where)/select_n | solution.py:538
  0.7 0.8 %slice_reduce_fusion = (u32[]{:T(128)}, u32[]{:T(128)}) fusion(u32[128,8]{0,1:T(8,128)S(1)} %compare_select_fusion), kind=kLoop, calls=%fused_computation.45 | loop fusion | flops 1022 | bytes 4104 | tf_op jit(solution)/shard_map/reduce_sum | solution.py:539
  6.6 44.0 %conditional.1 = (bf16[128,4096]{1,0:T(8,128)(2,1)S(1)}) conditional(s32[]{:T(128)} %convert_element_type.31, (s32[1]{0:T(128)}, s32[1,8]{1,0:T(1,128)}, s32[1,8]{1,0:T(1,128)}, s32[128,8]{0,1:T(8,128)}, bf16[256,1,4096]{2,0,1:T(8,128)(2,1)}, /*index=5*/bf16[4096,512]{1,0:T(8,128)(2,1)}, bf16[4096,512]{1,0:T(8,128)(2,1)}, f32[128]{0:T(128)}, ...), branch_computations={%region_2.7_spmd, %region_7.8_spmd} | conditional | flops 4592182784 | bytes 141282944 | solution.py:544
  6.8 43.8 %fused_cross_attention.1 = bf16[128,4096]{1,0:T(8,128)(2,1)S(1)} custom-call(bf16[128,4096]{1,0:T(8,128)(2,1)} %get-tuple-element.58.q_hbm, bf16[256,4096]{1,0:T(8,128)(2,1)} %bitcast.66, bf16[4096,512]{1,0:T(8,128)(2,1)} %get-tuple-element.60.wk_hbm, bf16[4096,512]{1,0:T(8,128)(2,1)} %get-tuple-element.61.wv_hbm, f32[1,128]{1,0:T(1,128)} %bitcast.72, ...), custom_call_target="tpu_custom_call" | custom-call | tf_op jit(solution)/shard_map/cond/branch_1_fun/fused_cross_attention/pallas_call | solution.py:478
  50.7 1.0 %copy.116 = bf16[128,4096]{1,0:T(8,128)(2,1)} copy(bf16[128,4096]{1,0:T(8,128)(2,1)S(1)} %get-tuple-element.135) | data formatting | bytes 2097152
  (1 shorter events, 0.0 us)

commit v4 on v3

--- a/solution.py
+++ b/solution.py
@@ -19,7 +19,7 @@
 MESH = pl.DeviceIdType.MESH
 MASKED = -32768.0
 PIECES = 8
-UNROLL = 4
+AHEAD = 3
 Z_STEPS = (0, 1, 7, 2, 6, 3, 5, 4)
 
 epsilon = 1e-05
@@ -136,7 +136,8 @@
     send2,
     recv2,
     q_send,
-    q_all,
+    q_own,
+    q_sib,
     q_tail,
     k_tail,
     o_sum,
@@ -158,7 +159,7 @@
     sibling = 1 - core
     z, p = doc // PLANE, doc % PLANE
     px, py = p // 4, p % 4
-    tokens = q_v.shape[0]
+    tokens, width = q_v.shape
     n_slots, depth = x_v.shape
     piece = depth // PIECES
     row_block = n_slots // 4
@@ -179,10 +180,9 @@
 
     for i in range(4):
         x_copy(i).start()
-    for c in range(PIECES):
+    for c in range(AHEAD):
         w_copy(0, c).start()
         w_copy(1, c).start()
-    q_copy.start()
 
     def z_to(s):
         return (z + Z_STEPS[s]) % PLANES
@@ -229,28 +229,15 @@
     goes_to = jnp.sum(found, axis=0, keepdims=True) - 1.0
     pick1[...] = flag(iota((PLANES * CAPACITY, n_slots), 0).astype(jnp.float32) == goes_to)
 
-    pair = 2 * IMG_MAX
-    rows_e, cols_e = PLANE * pair, 2 * CAPACITY
-    row_step = iota((rows_e, 128), 0) // pair
-    row_doc = z * PLANE + ((px + row_step // 4) % 4) * 4 + (py + row_step % 4) % 4
-    mine_doc = flag(iota((rows_e, 128), 1) == row_doc)
-    rank_plus = jnp.where(present, rank + 1.0, 0.0).astype(jnp.bfloat16)
-    by_slot = mm(mine_doc, rank_plus, RIGHT)
-    chosen = iota((rows_e, IMG_MAX), 1) == iota((rows_e, IMG_MAX), 0) % IMG_MAX
-    row_rank = jnp.sum(jnp.where(chosen, by_slot, 0.0), axis=1, keepdims=True)
-    source = (iota((rows_e, 1), 0) // IMG_MAX) % 2
-    row_target = jnp.where(row_rank > 0.0, row_rank - 1.0 + (CAPACITY * source).astype(jnp.float32), -1.0)
-    expand[...] = flag(iota((rows_e, cols_e), 1).astype(jnp.float32) == row_target)
-
     lane = iota((1, HEAD_SIZE), 1)
     first_t = jnp.zeros((1, HEAD_SIZE), jnp.int32)
     last_t = jnp.zeros((1, HEAD_SIZE), jnp.int32)
     for j in range(IMG_MAX):
         first_t = jnp.where(lane == j, pos_ref[0, j], first_t)
         last_t = jnp.where(lane == j, end_ref[0, j], last_t)
-    block = iota((2 * tokens, HEAD_SIZE), 0) // tokens
+    block = iota((4 * tokens, HEAD_SIZE), 0) // (2 * tokens)
     owner = jnp.where(block == 0, core, sibling)
-    t_pos = owner * tokens + iota((2 * tokens, HEAD_SIZE), 0) % tokens
+    t_pos = owner * tokens + iota((4 * tokens, HEAD_SIZE), 0) % tokens
     attends = (lane < count_ref[0]) & (first_t <= t_pos) & (t_pos < last_t)
     q_tail[...] = flag(jnp.logical_not(attends))
     n_keys = k_tail.shape[0]
@@ -264,6 +251,10 @@
         cols = pl.ds(c * piece, piece)
         for i, (w, total) in enumerate(((wk_v, sum_k), (wv_v, sum_v))):
             w_copy(i, c).wait()
+            if c + AHEAD < PIECES:
+                w_copy(i, c + AHEAD).start()
+            elif c + AHEAD == PIECES and i == 0:
+                q_copy.start()
             term = mm(x_v[:, cols], w[cols, :])
             total[...] = term if c == 0 else total[...] + term
 
@@ -286,25 +277,27 @@
     q_gain = qg_ref[...]
     half_width = QUERY_HEADS // 2 * HEAD_SIZE
 
-    def norm_queries(i, carry):
-        at = pl.multiple_of(i * HEAD_SIZE, HEAD_SIZE)
-        own_cols = pl.ds(pl.multiple_of(core * half_width + at, HEAD_SIZE), HEAD_SIZE)
-        sib_cols = pl.ds(pl.multiple_of(sibling * half_width + at, HEAD_SIZE), HEAD_SIZE)
-        q_all[0, :, pl.ds(at, HEAD_SIZE)] = head_norm(q_v[:, own_cols].astype(jnp.float32), q_gain).astype(jnp.bfloat16)
-        q_send[:, pl.ds(at, HEAD_SIZE)] = head_norm(q_v[:, sib_cols].astype(jnp.float32), q_gain).astype(jnp.bfloat16)
+    def norm_queries(n, carry):
+        for u in range(4):
+            i = n * 4 + u
+            at = pl.multiple_of(i * HEAD_SIZE, HEAD_SIZE)
+            own_cols = pl.ds(pl.multiple_of(core * half_width + at, HEAD_SIZE), HEAD_SIZE)
+            sib_cols = pl.ds(pl.multiple_of(sibling * half_width + at, HEAD_SIZE), HEAD_SIZE)
+            q_own[i] = head_norm(q_v[:, own_cols].astype(jnp.float32), q_gain).astype(jnp.bfloat16)
+            q_send[i] = head_norm(q_v[:, sib_cols].astype(jnp.float32), q_gain).astype(jnp.bfloat16)
         return carry
 
-    def norm_all_queries():
-        lax.fori_loop(0, QUERY_HEADS // 2, norm_queries, 0)
-
+    lax.fori_loop(0, QUERY_HEADS // 8, norm_queries, 0)
     q_exchange = pltpu.make_async_remote_copy(
         src_ref=q_send,
-        dst_ref=q_all.at[1],
+        dst_ref=q_sib,
         send_sem=q_sems.at[0],
         recv_sem=q_sems.at[1],
         device_id=(doc, sibling),
         device_id_type=MESH,
     )
+
+    q_exchange.start()
 
     def hop1(s):
         return pltpu.make_async_remote_copy(
@@ -343,8 +336,18 @@
         send1[s] = packed[s]
     for s in range(1, PLANES):
         hop1(s).start()
-    norm_all_queries()
-    q_exchange.start()
+    pair = 2 * IMG_MAX
+    rows_e, cols_e = PLANE * pair, 2 * CAPACITY
+    row_step = iota((rows_e, 128), 0) // pair
+    row_doc = z * PLANE + ((px + row_step // 4) % 4) * 4 + (py + row_step % 4) % 4
+    mine_doc = flag(iota((rows_e, 128), 1) == row_doc)
+    rank_plus = jnp.where(present, rank + 1.0, 0.0).astype(jnp.bfloat16)
+    by_slot = mm(mine_doc, rank_plus, RIGHT)
+    chosen = iota((rows_e, IMG_MAX), 1) == iota((rows_e, IMG_MAX), 0) % IMG_MAX
+    row_rank = jnp.sum(jnp.where(chosen, by_slot, 0.0), axis=1, keepdims=True)
+    source = (iota((rows_e, 1), 0) // IMG_MAX) % 2
+    row_target = jnp.where(row_rank > 0.0, row_rank - 1.0 + (CAPACITY * source).astype(jnp.float32), -1.0)
+    expand[...] = flag(iota((rows_e, cols_e), 1).astype(jnp.float32) == row_target)
 
     def expand_and_send(k):
         for s in (2 * k, 2 * k + 1):
@@ -365,46 +368,54 @@
     scale = 1.0 / math.sqrt(HEAD_SIZE)
     last = PLANES // 2 - 1
 
+    blocks = GROUP
+    per_head = blocks // 2
+
     def attend(k):
         await_group(recv2, k, r2_sem)
 
-        def heads(n, carry):
-            h = n // (GROUP // UNROLL)
-            k_cols = pl.ds(pl.multiple_of(h * HEAD_SIZE, HEAD_SIZE), HEAD_SIZE)
-            v_cols = pl.ds(pl.multiple_of(half + h * HEAD_SIZE, HEAD_SIZE), HEAD_SIZE)
-            keys = jnp.concatenate([recv2[k, :, :, k_cols].reshape(n_keys, HEAD_SIZE), k_tail[...]], axis=1)
-            values = jnp.concatenate([recv2[k, :, :, v_cols].reshape(n_keys, HEAD_SIZE), ones], axis=1)
-            for u in range(UNROLL):
-                g = n * UNROLL + u
-                cols = pl.ds(pl.multiple_of(g * HEAD_SIZE, HEAD_SIZE), HEAD_SIZE)
-                q = q_all[:, :, cols].reshape(2 * tokens, HEAD_SIZE)
-                scores = mm(jnp.concatenate([q, q_tail[...]], axis=1), keys, RIGHT)
-                weights = jnp.exp(scores * scale).astype(jnp.bfloat16)
-                mixed = mm(weights, values)
-                if k > 0:
-                    mixed = mixed + o_sum[g]
-                if k < last:
-                    o_sum[g] = mixed
-                else:
-                    total = mixed[:, HEAD_SIZE:]
-                    out = (mixed[:, :HEAD_SIZE] / jnp.where(total > 0.0, total, 1.0)).astype(jnp.bfloat16)
-                    o_own[:, cols] = out[:tokens]
-                    o_send[:, cols] = out[tokens:]
-            return carry
-
-        per_head = GROUP // UNROLL
-        if k < last:
-            lax.fori_loop(0, 2 * per_head, heads, 0)
-        else:
-            for h in range(2):
-                lax.fori_loop(h * per_head, (h + 1) * per_head, heads, 0)
-                o_copy(h).start()
-                own_copy(h).start()
-
-    out_width = GROUP * HEAD_SIZE
+        def keys_of(b):
+            at = (b // per_head) * HEAD_SIZE
+            rows = recv2[k, :, :, at : at + HEAD_SIZE].reshape(n_keys, HEAD_SIZE)
+            return jnp.concatenate([rows, k_tail[...]], axis=1)
+
+        def values_of(b):
+            at = half + (b // per_head) * HEAD_SIZE
+            rows = recv2[k, :, :, at : at + HEAD_SIZE].reshape(n_keys, HEAD_SIZE)
+            return jnp.concatenate([rows, ones], axis=1)
+
+        def scores_of(b):
+            own = q_own[2 * b : 2 * b + 2].reshape(2 * tokens, HEAD_SIZE)
+            sib = q_sib[2 * b : 2 * b + 2].reshape(2 * tokens, HEAD_SIZE)
+            rows = jnp.concatenate([jnp.concatenate([own, sib], axis=0), q_tail[...]], axis=1)
+            return mm(rows, keys_of(b), RIGHT)
+
+        scores = scores_of(0)
+        for b in range(blocks):
+            weights = jnp.exp(scores * scale).astype(jnp.bfloat16)
+            if b + 1 < blocks:
+                scores = scores_of(b + 1)
+            mixed = mm(weights, values_of(b))
+            if k > 0:
+                mixed = mixed + o_sum[b]
+            if k < last:
+                o_sum[b] = mixed
+                continue
+            total = mixed[:, HEAD_SIZE:]
+            out = (mixed[:, :HEAD_SIZE] / jnp.where(total > 0.0, total, 1.0)).astype(jnp.bfloat16)
+            for i in range(2):
+                at = (2 * b + i) * HEAD_SIZE
+                o_own[:, at : at + HEAD_SIZE] = out[i * tokens : (i + 1) * tokens]
+                o_send[:, at : at + HEAD_SIZE] = out[(2 + i) * tokens : (3 + i) * tokens]
+            if b % 2 == 1:
+                o_copy(b // 2).start()
+                own_copy(b // 2).start()
+
+    quarters = 4
+    out_width = width // 2 // quarters
 
     def out_at(of, h):
-        return out_hbm.at[:, pl.ds(pl.multiple_of((of * 2 + h) * out_width, out_width), out_width)]
+        return out_hbm.at[:, pl.ds(pl.multiple_of((of * quarters + h) * out_width, out_width), out_width)]
 
     def o_copy(h):
         return pltpu.make_async_remote_copy(
@@ -446,7 +457,7 @@
     for k in range(last + 1):
         await_group(send2, k, s2_sem)
     q_exchange.wait_send()
-    for h in range(2):
+    for h in range(quarters):
         o_copy(h).wait_send()
         own_copy(h).wait()
         o_in(h).wait_recv()
@@ -495,19 +506,20 @@
             pltpu.VMEM((PLANES, CAPACITY, 2 * two), bf16),
             pltpu.VMEM((groups, PLANE, pair, 2 * two), bf16),
             pltpu.VMEM((groups, PLANE, pair, 2 * two), bf16),
-            pltpu.VMEM((tokens, width // 2), bf16),
-            pltpu.VMEM((2, tokens, width // 2), bf16),
-            pltpu.VMEM((2 * tokens, HEAD_SIZE), bf16),
+            pltpu.VMEM((QUERY_HEADS // 2, tokens, HEAD_SIZE), bf16),
+            pltpu.VMEM((QUERY_HEADS // 2, tokens, HEAD_SIZE), bf16),
+            pltpu.VMEM((QUERY_HEADS // 2, tokens, HEAD_SIZE), bf16),
+            pltpu.VMEM((4 * tokens, HEAD_SIZE), bf16),
             pltpu.VMEM((PLANE * pair, HEAD_SIZE), bf16),
-            pltpu.VMEM((2 * GROUP, 2 * tokens, two), f32),
+            pltpu.VMEM((GROUP, 4 * tokens, two), f32),
             pltpu.VMEM((tokens, width // 2), bf16),
             pltpu.VMEM((tokens, width // 2), bf16),
             dma((5,)),
             dma((2, PIECES)),
-            dma((2,)),
+            dma((4,)),
             dma((2, 2)),
             dma((2,)),
-            dma((2, 2)),
+            dma((2, 4)),
             dma((PLANES,)),
             dma((PLANES,)),
             dma((groups,)),
@@ -532,16 +544,23 @@
     return out
 
 
+def fits_kernel(slot_ref, fits_ref):
+    same = (iota((128, 128), 0) // PLANE) == (iota((128, 128), 1) // PLANE)
+    totals = mm(flag(slot_ref[...] >= 0), flag(same))
+    crowded = jnp.max(jnp.sum(totals, axis=0, keepdims=True))
+    fits_ref[0] = jnp.where(crowded <= CAPACITY, 1, 0)
+
+
 def shards(*arrays):
     image_slot = arrays[7]
-    shift = 8 * (jnp.arange(image_slot.shape[0], dtype=jnp.uint32) // PLANE % 4)
-    part = jnp.where(image_slot >= 0, jnp.uint32(1) << shift[:, None], jnp.uint32(0))
-    words = [jnp.sum(part[: 4 * PLANE]), jnp.sum(part[4 * PLANE :])]
-    fits = jnp.bool_(True)
-    for word in words:
-        for i in range(4):
-            fits = fits & (((word >> (8 * i)) & 255) <= CAPACITY)
-    return lax.cond(fits, packed_route, general_route, *arrays)
+    fits = pl.pallas_call(
+        fits_kernel,
+        out_shape=jax.ShapeDtypeStruct((1,), jnp.int32),
+        in_specs=[pl.BlockSpec(memory_space=pltpu.VMEM)],
+        out_specs=pl.BlockSpec(memory_space=pltpu.SMEM),
+        name="fits",
+    )(image_slot.T)
+    return lax.cond(fits[0] > 0, packed_route, general_route, *arrays)
 
 def solution(mesh):
     in_specs = (

time: 51.8 us -> 44.5 us (0.86)
  between operations: 5.15 us -> 0.67 us
  other arithmetic: 1.46 us -> 0 us
  Pallas kernels: 43.8 us -> 42.4 us
    pallas_call x1, Pallas kernels: 43.8 us -> 40.9 us  [packed_route(): pl.pallas_call(fused_kernel, out_shape=jax.ShapeDtypeStruct((tokens, widt...]
    pallas_call x0 -> x1, Pallas kernels: none -> 1.45 us  [shards(): pl.pallas_call(fits_kernel, out_shape=jax.ShapeDtypeStruct((1,), jnp.int3...]
    reduce_sum x1 -> x0, other arithmetic: 0.77 us -> none  [shards(): words = [jnp.sum(part[:4 * PLANE]), jnp.sum(part[4 * PLANE:])]]
    select_n x1 -> x0, other arithmetic: 0.69 us -> none  [shards(): jnp.where(image_slot >= 0, jnp.uint32(1) << shift[:, None], jnp.uint32(0))]
where the time goes in v4:
time: 44.5 us; the launch traced here: 44.3 us
  Pallas kernels  42.4 us (95%)
  local copies, waits for them, and re-layouts  0.97 us (2%)
  between operations  0.67 us (2%)
    pallas_call x1, Pallas kernels, packed_route(): pl.pallas_call(fused_kernel, out_shape=jax.ShapeDtypeStruct((tokens, widt...  40.9 us
    pallas_call x1, Pallas kernels, shards(): pl.pallas_call(fits_kernel, out_shape=jax.ShapeDtypeStruct((1,), jnp.int3...  1.45 us
    unnamed x1, local copies, waits for them, and re-layouts  0.97 us

profile of v4, /device:TPU:1, one launch (start us, length us, event | category | flops | bytes accessed | tf_op | source)
XLA Modules:
  0.0 44.3 jit_solution(3026872221391144952)
XLA Ops:
  0.0 1.5 %fits.1 = s32[1]{0:T(128)} custom-call(s32[8,128]{1,0:T(8,128)} %bitcast.72), custom_call_target="tpu_custom_call" | custom-call | tf_op jit(solution)/shard_map/fits/pallas_call | solution.py:556
  2.1 41.2 %conditional.1 = (bf16[128,4096]{1,0:T(8,128)(2,1)S(1)}) conditional(s32[]{:T(128)} %bitcast.20, (s32[1]{0:T(128)}, s32[1,8]{1,0:T(1,128)}, s32[1,8]{1,0:T(1,128)}, s32[128,8]{0,1:T(8,128)}, bf16[256,1,4096]{2,0,1:T(8,128)(2,1)}, /*index=5*/bf16[4096,512]{1,0:T(8,128)(2,1)}, bf16[4096,512]{1,0:T(8,128)(2,1)}, f32[128]{0:T(128)}, ...), branch_computations={%region_0.5_spmd, %region_5.6_spmd} | conditional | flops 4592182784 | bytes 141282944 | solution.py:563
  2.4 40.9 %fused_cross_attention.1 = bf16[128,4096]{1,0:T(8,128)(2,1)S(1)} custom-call(bf16[128,4096]{1,0:T(8,128)(2,1)} %get-tuple-element.58.q_hbm, bf16[256,4096]{1,0:T(8,128)(2,1)} %bitcast.68, bf16[4096,512]{1,0:T(8,128)(2,1)} %get-tuple-element.60.wk_hbm, bf16[4096,512]{1,0:T(8,128)(2,1)} %get-tuple-element.61.wv_hbm, f32[1,128]{1,0:T(1,128)} %bitcast.75, ...), custom_call_target="tpu_custom_call" | custom-call | tf_op jit(solution)/shard_map/cond/branch_1_fun/fused_cross_attention/pallas_call | solution.py:489
  43.3 1.0 %copy.116 = bf16[128,4096]{1,0:T(8,128)(2,1)} copy(bf16[128,4096]{1,0:T(8,128)(2,1)S(1)} %get-tuple-element.135) | data formatting | bytes 2097152

commit v5 on v4

--- a/solution.py
+++ b/solution.py
@@ -16,11 +16,13 @@
 PLANE = 16
 PLANES = 8
 CAPACITY = 48
+SIDE = 4
+GROUP_CAPACITY = 16
 MESH = pl.DeviceIdType.MESH
 MASKED = -32768.0
 PIECES = 8
 AHEAD = 3
-Z_STEPS = (0, 1, 7, 2, 6, 3, 5, 4)
+Z_ORDER = (0, 1, 7, 2, 6, 3, 5, 4)
 
 epsilon = 1e-05
 
@@ -109,6 +111,10 @@
 RIGHT = ((1,), (1,))
 
 
+def z_slot_of(plane):
+    return jnp.where(plane == 0, 0, jnp.where(plane <= PLANES // 2, 2 * plane - 1, 2 * (PLANES - plane)))
+
+
 def fused_kernel(
     q_hbm,
     x_hbm,
@@ -130,9 +136,12 @@
     got_k,
     got_v,
     pick1,
+    pick2,
     expand,
     send1,
     recv1,
+    send_a,
+    recv_a,
     send2,
     recv2,
     q_send,
@@ -151,6 +160,8 @@
     o_sems,
     s1_sem,
     r1_sem,
+    sa_sem,
+    ra_sem,
     s2_sem,
     r2_sem,
 ):
@@ -158,7 +169,11 @@
     core = lax.axis_index("seq")
     sibling = 1 - core
     z, p = doc // PLANE, doc % PLANE
-    px, py = p // 4, p % 4
+    px, py = p // SIDE, p % SIDE
+    a = jnp.where(core == 0, px, py)
+    b = jnp.where(core == 0, py, px)
+    step_a = 1 + (SIDE - 1) * (1 - core)
+    step_b = 1 + (SIDE - 1) * core
     tokens, width = q_v.shape
     n_slots, depth = x_v.shape
     piece = depth // PIECES
@@ -184,11 +199,13 @@
         w_copy(0, c).start()
         w_copy(1, c).start()
 
-    def z_to(s):
-        return (z + Z_STEPS[s]) % PLANES
-
-    def plane_to(i):
-        return ((px + i // 4) % 4) * 4 + (py + i % 4) % 4
+    own_slot = z_slot_of(z)
+
+    def along_a(i):
+        return (a + i) % SIDE * step_a + b * step_b
+
+    def along_b(i):
+        return a * step_a + (b + i) % SIDE * step_b
 
     barrier = pltpu.get_barrier_semaphore()
     pl.semaphore_signal(barrier, inc=1, device_id=(doc, sibling), device_id_type=MESH)
@@ -198,27 +215,28 @@
         pl.semaphore_signal(barrier, inc=1, device_id=(there, core), device_id_type=MESH)
         return carry
 
-    def greet_plane(i, carry):
-        pl.semaphore_signal(barrier, inc=1, device_id=(z * PLANE + plane_to(i), core), device_id_type=MESH)
-        return carry
-
     lax.fori_loop(1, PLANES, greet_z, 0)
-    lax.fori_loop(1, PLANE, greet_plane, 0)
+    for i in range(1, SIDE):
+        for near in (along_a(i), along_b(i)):
+            pl.semaphore_signal(barrier, inc=1, device_id=(z * PLANE + near, core), device_id_type=MESH)
 
     slots_t = slot_ref[...]
     present = slots_t >= 0
     there = flag(present)
     d_row, d_col = iota((128, 128), 0), iota((128, 128), 1)
     same = (d_row // PLANE) == (d_col // PLANE)
-    before = mm(there, flag(same & (d_row < d_col)))
-    totals = mm(there, flag(same)).astype(jnp.bfloat16)
-    earlier = mm(flag(iota((8, 8), 1) < iota((8, 8), 0)), totals)
-    rank = before + earlier
+    first_order = flag(iota((8, 8), 1) < iota((8, 8), 0))
+
+    def rank_within(same):
+        before = mm(there, flag(same & (d_row < d_col)))
+        totals = mm(there, flag(same)).astype(jnp.bfloat16)
+        return before + mm(first_order, totals)
+
+    rank = rank_within(same)
     identity = flag(d_row == d_col)
     slot_cols = mm(identity, slots_t.astype(jnp.float32).astype(jnp.bfloat16), RIGHT)
     rank_cols = mm(identity, jnp.where(present, rank, 0.0).astype(jnp.bfloat16), RIGHT)
-    away = (iota((128, 1), 0) // PLANE + PLANES - z) % PLANES
-    z_slot = jnp.where(away == 0, 0, jnp.where(away <= PLANES // 2, 2 * away - 1, 2 * (PLANES - away)))
+    z_slot = z_slot_of(iota((128, 1), 0) // PLANE)
     plane_base = (CAPACITY * z_slot).astype(jnp.float32) + 1.0
     slot_lane = iota((1, n_slots), 1).astype(jnp.float32)
     found = jnp.zeros((128, n_slots), jnp.float32)
@@ -269,7 +287,7 @@
             device_id_type=MESH,
         )
 
-    pl.semaphore_wait(barrier, PLANES - 1 + PLANE - 1 + 1)
+    pl.semaphore_wait(barrier, PLANES - 1 + 2 * (SIDE - 1) + 1)
     part_copy(0).start()
     part_copy(1).start()
 
@@ -302,12 +320,25 @@
     def hop1(s):
         return pltpu.make_async_remote_copy(
             src_ref=send1.at[s],
+            dst_ref=recv1.at[own_slot],
+            send_sem=s1_sem.at[s],
+            recv_sem=r1_sem.at[own_slot],
+            device_id=(Z_ORDER[s] * PLANE + p, core),
+            device_id_type=MESH,
+        )
+
+    def hop1_in(s):
+        return pltpu.make_async_remote_copy(
+            src_ref=send1.at[s],
             dst_ref=recv1.at[s],
             send_sem=s1_sem.at[s],
             recv_sem=r1_sem.at[s],
-            device_id=(z_to(s) * PLANE + p, core),
+            device_id=(Z_ORDER[s] * PLANE + p, core),
             device_id_type=MESH,
         )
+
+    def if_other(s, act):
+        pl.when(own_slot != s)(act)
 
     def hop2(k, i):
         return pltpu.make_async_remote_copy(
@@ -315,12 +346,22 @@
             dst_ref=recv2.at[k, i],
             send_sem=s2_sem.at[k],
             recv_sem=r2_sem.at[k],
-            device_id=(z * PLANE + plane_to(i), core),
+            device_id=(z * PLANE + along_b(i), core),
             device_id_type=MESH,
         )
 
+    def hop_a(k, i):
+        return pltpu.make_async_remote_copy(
+            src_ref=send_a.at[k, i],
+            dst_ref=recv_a.at[k, i],
+            send_sem=sa_sem.at[k],
+            recv_sem=ra_sem.at[k],
+            device_id=(z * PLANE + along_a(i), core),
+            device_id_type=MESH,
+        )
+
     def await_group(ref, k, sem):
-        part = ref.at[k, pl.ds(1, PLANE - 1)]
+        part = ref.at[k, pl.ds(1, SIDE - 1)]
         pltpu.make_async_copy(part, part, sem.at[k]).wait()
 
     key_gain = kg_ref[...]
@@ -331,38 +372,60 @@
     raw_v = (sum_v[:, own_half] + got_v[...]).astype(jnp.bfloat16)
     kv_own = jnp.concatenate(keys_own + [raw_v], axis=1)
     packed = mm(pick1[...], kv_own).astype(jnp.bfloat16).reshape(PLANES, CAPACITY, 2 * half)
-    recv1[0] = packed[0]
-    for s in range(1, PLANES):
-        send1[s] = packed[s]
-    for s in range(1, PLANES):
-        hop1(s).start()
-    pair = 2 * IMG_MAX
-    rows_e, cols_e = PLANE * pair, 2 * CAPACITY
-    row_step = iota((rows_e, 128), 0) // pair
-    row_doc = z * PLANE + ((px + row_step // 4) % 4) * 4 + (py + row_step % 4) % 4
+    send1[...] = packed
+    for s in range(PLANES):
+        if_other(s, lambda s=s: hop1(s).start())
+    recv1[own_slot] = send1[own_slot]
+    def a_of(doc_ids):
+        return jnp.where(core == 0, doc_ids % PLANE // SIDE, doc_ids % SIDE)
+
+    group_rank = rank_within(same & (a_of(d_row) == a_of(d_col)))
+    d_lane = iota((1, 128), 1)
+    a_step = (a_of(d_lane) + SIDE - a) % SIDE
+    rows_p, cols_p = SIDE * 2 * GROUP_CAPACITY, 2 * CAPACITY
+    row_p = iota((rows_p, 1), 0)
+    row_key = (row_p // (2 * GROUP_CAPACITY) * GROUP_CAPACITY + row_p % GROUP_CAPACITY).astype(jnp.float32)
+    entry_key = jnp.where(
+        present & (d_lane // PLANE == z), (a_step * GROUP_CAPACITY).astype(jnp.float32) + group_rank, -1.0
+    )
+    hits = jnp.zeros((rows_p, 128), jnp.float32)
+    for j in range(IMG_MAX):
+        hits = hits + jnp.where(entry_key[j : j + 1] == row_key, rank[j : j + 1] + 1.0, 0.0)
+    plane_rank = jnp.sum(hits, axis=1, keepdims=True)
+    source = (CAPACITY * (row_p // GROUP_CAPACITY % 2)).astype(jnp.float32)
+    row_target = jnp.where(plane_rank > 0.0, plane_rank - 1.0 + source, -1.0)
+    pick2[...] = flag(iota((rows_p, cols_p), 1).astype(jnp.float32) == row_target)
+
+    per_step = 2 * SIDE * IMG_MAX
+    rows_e, cols_e = SIDE * per_step, 2 * SIDE * GROUP_CAPACITY
+    row_doc = z * PLANE + a * step_a + (b + iota((rows_e, 128), 0) // per_step) % SIDE * step_b
     mine_doc = flag(iota((rows_e, 128), 1) == row_doc)
-    rank_plus = jnp.where(present, rank + 1.0, 0.0).astype(jnp.bfloat16)
+    rank_plus = jnp.where(present, group_rank + 1.0, 0.0).astype(jnp.bfloat16)
     by_slot = mm(mine_doc, rank_plus, RIGHT)
     chosen = iota((rows_e, IMG_MAX), 1) == iota((rows_e, IMG_MAX), 0) % IMG_MAX
     row_rank = jnp.sum(jnp.where(chosen, by_slot, 0.0), axis=1, keepdims=True)
-    source = (iota((rows_e, 1), 0) // IMG_MAX) % 2
-    row_target = jnp.where(row_rank > 0.0, row_rank - 1.0 + (CAPACITY * source).astype(jnp.float32), -1.0)
+    source = (iota((rows_e, 1), 0) // IMG_MAX) % (2 * SIDE)
+    row_target = jnp.where(row_rank > 0.0, row_rank - 1.0 + (GROUP_CAPACITY * source).astype(jnp.float32), -1.0)
     expand[...] = flag(iota((rows_e, cols_e), 1).astype(jnp.float32) == row_target)
 
+    def pick_and_send(k):
+        for s in (2 * k, 2 * k + 1):
+            if_other(s, lambda s=s: hop1_in(s).wait_recv())
+        rows = mm(pick2[...], recv1[pl.ds(2 * k, 2)].reshape(2 * CAPACITY, 2 * half)).astype(jnp.bfloat16)
+        rows = rows.reshape(SIDE, 2 * GROUP_CAPACITY, 2 * half)
+        recv_a[k, 0] = rows[0]
+        send_a[k, pl.ds(1, SIDE - 1)] = rows[1:]
+        for i in range(1, SIDE):
+            hop_a(k, i).start()
+
     def expand_and_send(k):
-        for s in (2 * k, 2 * k + 1):
-            if s > 0:
-                hop1(s).wait_recv()
-        rows = mm(expand[...], recv1[pl.ds(2 * k, 2)].reshape(2 * CAPACITY, 2 * half)).astype(jnp.bfloat16)
-        rows = rows.reshape(PLANE, pair, 2 * half)
+        await_group(recv_a, k, ra_sem)
+        rows = mm(expand[...], recv_a[k].reshape(cols_e, 2 * half)).astype(jnp.bfloat16)
+        rows = rows.reshape(SIDE, per_step, 2 * half)
         recv2[k, 0] = rows[0]
-        send2[k, pl.ds(1, PLANE - 1)] = rows[1:]
-
-        def body(i, carry):
+        send2[k, pl.ds(1, SIDE - 1)] = rows[1:]
+        for i in range(1, SIDE):
             hop2(k, i).start()
-            return carry
-
-        lax.fori_loop(1, PLANE, body, 0)
 
     ones = jnp.ones((n_keys, HEAD_SIZE), jnp.bfloat16)
     scale = 1.0 / math.sqrt(HEAD_SIZE)
@@ -440,21 +503,26 @@
     def own_copy(h):
         return pltpu.make_async_copy(o_own.at[:, pl.ds(h * out_width, out_width)], out_at(core, h), out_sem.at[h])
 
+    pick_and_send(0)
+    pick_and_send(1)
     expand_and_send(0)
+    pick_and_send(2)
     expand_and_send(1)
-    expand_and_send(2)
     q_exchange.wait_recv()
     attend(0)
+    pick_and_send(3)
+    expand_and_send(2)
+    attend(1)
     expand_and_send(3)
-    attend(1)
     attend(2)
     attend(3)
 
     for i in range(2):
         part_copy(i).wait_send()
-    for s in range(1, PLANES):
-        hop1(s).wait_send()
+    for s in range(PLANES):
+        if_other(s, lambda s=s: hop1(s).wait_send())
     for k in range(last + 1):
+        await_group(send_a, k, sa_sem)
         await_group(send2, k, s2_sem)
     q_exchange.wait_send()
     for h in range(quarters):
@@ -485,7 +553,7 @@
     bf16, f32 = jnp.bfloat16, jnp.float32
     dma = pltpu.SemaphoreType.DMA
     groups = PLANES // 2
-    pair = 2 * IMG_MAX
+    keys = 2 * PLANE * IMG_MAX
     out = pl.pallas_call(
         fused_kernel,
         out_shape=jax.ShapeDtypeStruct((tokens, width), bf16),
@@ -501,16 +569,19 @@
             pltpu.VMEM((n_slots, two), f32),
             pltpu.VMEM((n_slots, two), f32),
             pltpu.VMEM((PLANES * CAPACITY, n_slots), bf16),
-            pltpu.VMEM((PLANE * pair, 2 * CAPACITY), bf16),
+            pltpu.VMEM((SIDE * 2 * GROUP_CAPACITY, 2 * CAPACITY), bf16),
+            pltpu.VMEM((keys, 2 * SIDE * GROUP_CAPACITY), bf16),
             pltpu.VMEM((PLANES, CAPACITY, 2 * two), bf16),
             pltpu.VMEM((PLANES, CAPACITY, 2 * two), bf16),
-            pltpu.VMEM((groups, PLANE, pair, 2 * two), bf16),
-            pltpu.VMEM((groups, PLANE, pair, 2 * two), bf16),
+            pltpu.VMEM((groups, SIDE, 2 * GROUP_CAPACITY, 2 * two), bf16),
+            pltpu.VMEM((groups, SIDE, 2 * GROUP_CAPACITY, 2 * two), bf16),
+            pltpu.VMEM((groups, SIDE, keys // SIDE, 2 * two), bf16),
+            pltpu.VMEM((groups, SIDE, keys // SIDE, 2 * two), bf16),
             pltpu.VMEM((QUERY_HEADS // 2, tokens, HEAD_SIZE), bf16),
             pltpu.VMEM((QUERY_HEADS // 2, tokens, HEAD_SIZE), bf16),
             pltpu.VMEM((QUERY_HEADS // 2, tokens, HEAD_SIZE), bf16),
             pltpu.VMEM((4 * tokens, HEAD_SIZE), bf16),
-            pltpu.VMEM((PLANE * pair, HEAD_SIZE), bf16),
+            pltpu.VMEM((keys, HEAD_SIZE), bf16),
             pltpu.VMEM((GROUP, 4 * tokens, two), f32),
             pltpu.VMEM((tokens, width // 2), bf16),
             pltpu.VMEM((tokens, width // 2), bf16),
@@ -522,6 +593,8 @@
             dma((2, 4)),
             dma((PLANES,)),
             dma((PLANES,)),
+            dma((groups,)),
+            dma((groups,)),
             dma((groups,)),
             dma((groups,)),
         ],
@@ -545,10 +618,18 @@
 
 
 def fits_kernel(slot_ref, fits_ref):
-    same = (iota((128, 128), 0) // PLANE) == (iota((128, 128), 1) // PLANE)
-    totals = mm(flag(slot_ref[...] >= 0), flag(same))
-    crowded = jnp.max(jnp.sum(totals, axis=0, keepdims=True))
-    fits_ref[0] = jnp.where(crowded <= CAPACITY, 1, 0)
+    row, col = iota((128, 128), 0), iota((128, 128), 1)
+    there = flag(slot_ref[...] >= 0)
+    plane = row // PLANE == col // PLANE
+
+    def crowd(same):
+        return jnp.max(jnp.sum(mm(there, flag(same)), axis=0, keepdims=True))
+
+    in_plane = crowd(plane)
+    in_row = crowd(row // SIDE == col // SIDE)
+    in_column = crowd(plane & (row % SIDE == col % SIDE))
+    fits = (in_plane <= CAPACITY) & (in_row <= GROUP_CAPACITY) & (in_column <= GROUP_CAPACITY)
+    fits_ref[0] = jnp.where(fits, 1, 0)
 
 
 def shards(*arrays):

time: 44.5 us -> 49.7 us (1.12); the launches traced: 44.3 us -> 48.9 us
  Pallas kernels: 42.4 us -> 47 us
    pallas_call x1, Pallas kernels: 40.9 us -> 45.5 us  [packed_route(): pl.pallas_call(fused_kernel, out_shape=jax.ShapeDtypeStruct((tokens, widt...]
where the time goes in v5:
time: 49.7 us; the launch traced here: 48.9 us
  Pallas kernels  47 us (95%)
  local copies, waits for them, and re-layouts  0.97 us (2%)
  between operations  0.67 us (1%)
    pallas_call x1, Pallas kernels, packed_route(): pl.pallas_call(fused_kernel, out_shape=jax.ShapeDtypeStruct((tokens, widt...  45.5 us
    pallas_call x1, Pallas kernels, shards(): pl.pallas_call(fits_kernel, out_shape=jax.ShapeDtypeStruct((1,), jnp.int3...  1.47 us

profile of v5, /device:TPU:1, one launch (start us, length us, event | category | flops | bytes accessed | tf_op | source)
XLA Modules:
  0.0 48.9 jit_solution(17847053761218736131)
XLA Ops:
  0.0 1.5 %fits.1 = s32[1]{0:T(128)} custom-call(s32[8,128]{1,0:T(8,128)} %bitcast.72), custom_call_target="tpu_custom_call" | custom-call | tf_op jit(solution)/shard_map/fits/pallas_call | solution.py:637
  2.1 45.8 %conditional.1 = (bf16[128,4096]{1,0:T(8,128)(2,1)S(1)}) conditional(s32[]{:T(128)} %bitcast.20, (s32[1]{0:T(128)}, s32[1,8]{1,0:T(1,128)}, s32[1,8]{1,0:T(1,128)}, s32[128,8]{0,1:T(8,128)}, bf16[256,1,4096]{2,0,1:T(8,128)(2,1)}, /*index=5*/bf16[4096,512]{1,0:T(8,128)(2,1)}, bf16[4096,512]{1,0:T(8,128)(2,1)}, f32[128]{0:T(128)}, ...), branch_computations={%region_0.5_spmd, %region_5.6_spmd} | conditional | flops 4592182784 | bytes 141282944 | solution.py:644
  2.4 45.5 %fused_cross_attention.1 = bf16[128,4096]{1,0:T(8,128)(2,1)S(1)} custom-call(bf16[128,4096]{1,0:T(8,128)(2,1)} %get-tuple-element.58.q_hbm, bf16[256,4096]{1,0:T(8,128)(2,1)} %bitcast.68, bf16[4096,512]{1,0:T(8,128)(2,1)} %get-tuple-element.60.wk_hbm, bf16[4096,512]{1,0:T(8,128)(2,1)} %get-tuple-element.61.wv_hbm, f32[1,128]{1,0:T(1,128)} %bitcast.75, ...), custom_call_target="tpu_custom_call" | custom-call | tf_op jit(solution)/shard_map/cond/branch_1_fun/fused_cross_attention/pallas_call | solution.py:557
  47.9 1.0 %copy.116 = bf16[128,4096]{1,0:T(8,128)(2,1)} copy(bf16[128,4096]{1,0:T(8,128)(2,1)S(1)} %get-tuple-element.135) | data formatting | bytes 2097152

commit v6 on v4

--- a/solution.py
+++ b/solution.py
@@ -131,10 +131,14 @@
     got_v,
     pick1,
     expand,
+    pick_own,
+    expand_far,
     send1,
     recv1,
     send2,
     recv2,
+    send_one,
+    recv_one,
     q_send,
     q_own,
     q_sib,
@@ -153,6 +157,8 @@
     r1_sem,
     s2_sem,
     r2_sem,
+    so_sem,
+    ro_sem,
 ):
     doc = lax.axis_index("doc")
     core = lax.axis_index("seq")
@@ -229,6 +235,18 @@
     goes_to = jnp.sum(found, axis=0, keepdims=True) - 1.0
     pick1[...] = flag(iota((PLANES * CAPACITY, n_slots), 0).astype(jnp.float32) == goes_to)
 
+    def by_document(entries, rows, per_document):
+        step = iota((rows, 128), 0) // per_document
+        row_doc = z * PLANE + ((px + step // 4) % 4) * 4 + (py + step % 4) % 4
+        by_slot = mm(flag(iota((rows, 128), 1) == row_doc), entries.astype(jnp.bfloat16), RIGHT)
+        chosen = iota((rows, IMG_MAX), 1) == iota((rows, IMG_MAX), 0) % IMG_MAX
+        return jnp.sum(jnp.where(chosen, by_slot, 0.0), axis=1, keepdims=True)
+
+    rows_o = PLANE * IMG_MAX
+    slot_plus = jnp.where(present, (slots_t + 1).astype(jnp.float32), 0.0)
+    rank_plus = jnp.where(present, rank + 1.0, 0.0)
+    pick_own[...] = flag(iota((rows_o, n_slots), 1).astype(jnp.float32) == by_document(slot_plus, rows_o, IMG_MAX) - 1.0)
+
     lane = iota((1, HEAD_SIZE), 1)
     first_t = jnp.zeros((1, HEAD_SIZE), jnp.int32)
     last_t = jnp.zeros((1, HEAD_SIZE), jnp.int32)
@@ -331,35 +349,53 @@
     raw_v = (sum_v[:, own_half] + got_v[...]).astype(jnp.bfloat16)
     kv_own = jnp.concatenate(keys_own + [raw_v], axis=1)
     packed = mm(pick1[...], kv_own).astype(jnp.bfloat16).reshape(PLANES, CAPACITY, 2 * half)
-    recv1[0] = packed[0]
     for s in range(1, PLANES):
         send1[s] = packed[s]
     for s in range(1, PLANES):
         hop1(s).start()
+    def hop_one(n, i):
+        return pltpu.make_async_remote_copy(
+            src_ref=send_one.at[n, i],
+            dst_ref=recv_one.at[n, i],
+            send_sem=so_sem.at[n],
+            recv_sem=ro_sem.at[n],
+            device_id=(z * PLANE + plane_to(i), core),
+            device_id_type=MESH,
+        )
+
+    def send_single(n, rows):
+        rows = rows.reshape(PLANE, IMG_MAX, 2 * half)
+        rows = jnp.concatenate([rows[:, :, :half], rows[:, :, half:]], axis=1).astype(jnp.bfloat16)
+        recv_one[n, 0] = rows[0]
+        send_one[n, pl.ds(1, PLANE - 1)] = rows[1:]
+
+        def body(i, carry):
+            hop_one(n, PLANE - i).start()
+            return carry
+
+        lax.fori_loop(1, PLANE, body, 0)
+
+    send_single(0, mm(pick_own[...], kv_own))
     pair = 2 * IMG_MAX
     rows_e, cols_e = PLANE * pair, 2 * CAPACITY
-    row_step = iota((rows_e, 128), 0) // pair
-    row_doc = z * PLANE + ((px + row_step // 4) % 4) * 4 + (py + row_step % 4) % 4
-    mine_doc = flag(iota((rows_e, 128), 1) == row_doc)
-    rank_plus = jnp.where(present, rank + 1.0, 0.0).astype(jnp.bfloat16)
-    by_slot = mm(mine_doc, rank_plus, RIGHT)
-    chosen = iota((rows_e, IMG_MAX), 1) == iota((rows_e, IMG_MAX), 0) % IMG_MAX
-    row_rank = jnp.sum(jnp.where(chosen, by_slot, 0.0), axis=1, keepdims=True)
+    row_rank = by_document(rank_plus, rows_e, pair)
     source = (iota((rows_e, 1), 0) // IMG_MAX) % 2
     row_target = jnp.where(row_rank > 0.0, row_rank - 1.0 + (CAPACITY * source).astype(jnp.float32), -1.0)
+    expand_far[...] = flag(
+        iota((rows_o, CAPACITY), 1).astype(jnp.float32) == by_document(rank_plus, rows_o, IMG_MAX) - 1.0
+    )
     expand[...] = flag(iota((rows_e, cols_e), 1).astype(jnp.float32) == row_target)
 
     def expand_and_send(k):
-        for s in (2 * k, 2 * k + 1):
-            if s > 0:
-                hop1(s).wait_recv()
-        rows = mm(expand[...], recv1[pl.ds(2 * k, 2)].reshape(2 * CAPACITY, 2 * half)).astype(jnp.bfloat16)
+        for s in (2 * k + 1, 2 * k + 2):
+            hop1(s).wait_recv()
+        rows = mm(expand[...], recv1[pl.ds(2 * k + 1, 2)].reshape(2 * CAPACITY, 2 * half)).astype(jnp.bfloat16)
         rows = rows.reshape(PLANE, pair, 2 * half)
         recv2[k, 0] = rows[0]
         send2[k, pl.ds(1, PLANE - 1)] = rows[1:]
 
         def body(i, carry):
-            hop2(k, i).start()
+            hop2(k, PLANE - i).start()
             return carry
 
         lax.fori_loop(1, PLANE, body, 0)
@@ -372,7 +408,16 @@
     per_head = blocks // 2
 
     def attend(k):
-        await_group(recv2, k, r2_sem)
+        if k < last:
+            await_group(recv2, k, r2_sem)
+        else:
+            await_group(recv_one, 0, ro_sem)
+            await_group(recv_one, 1, ro_sem)
+            rows = recv_one[...].astype(jnp.float32)
+            keys = rows[:, :, :IMG_MAX].reshape(n_keys, half)
+            values = rows[:, :, IMG_MAX:].reshape(n_keys, half)
+            joined = jnp.concatenate([keys, values], axis=1).astype(jnp.bfloat16)
+            recv2[k] = joined.reshape(PLANE, pair, 2 * half)
 
         def keys_of(b):
             at = (b // per_head) * HEAD_SIZE
@@ -442,10 +487,11 @@
 
     expand_and_send(0)
     expand_and_send(1)
+    q_exchange.wait_recv()
     expand_and_send(2)
-    q_exchange.wait_recv()
     attend(0)
-    expand_and_send(3)
+    hop1(PLANES - 1).wait_recv()
+    send_single(1, mm(expand_far[...], recv1[PLANES - 1]))
     attend(1)
     attend(2)
     attend(3)
@@ -454,8 +500,10 @@
         part_copy(i).wait_send()
     for s in range(1, PLANES):
         hop1(s).wait_send()
-    for k in range(last + 1):
+    for k in range(last):
         await_group(send2, k, s2_sem)
+    await_group(send_one, 0, so_sem)
+    await_group(send_one, 1, so_sem)
     q_exchange.wait_send()
     for h in range(quarters):
         o_copy(h).wait_send()
@@ -502,10 +550,14 @@
             pltpu.VMEM((n_slots, two), f32),
             pltpu.VMEM((PLANES * CAPACITY, n_slots), bf16),
             pltpu.VMEM((PLANE * pair, 2 * CAPACITY), bf16),
+            pltpu.VMEM((PLANE * IMG_MAX, n_slots), bf16),
+            pltpu.VMEM((PLANE * IMG_MAX, CAPACITY), bf16),
             pltpu.VMEM((PLANES, CAPACITY, 2 * two), bf16),
             pltpu.VMEM((PLANES, CAPACITY, 2 * two), bf16),
             pltpu.VMEM((groups, PLANE, pair, 2 * two), bf16),
             pltpu.VMEM((groups, PLANE, pair, 2 * two), bf16),
+            pltpu.VMEM((2, PLANE, pair, two), bf16),
+            pltpu.VMEM((2, PLANE, pair, two), bf16),
             pltpu.VMEM((QUERY_HEADS // 2, tokens, HEAD_SIZE), bf16),
             pltpu.VMEM((QUERY_HEADS // 2, tokens, HEAD_SIZE), bf16),
             pltpu.VMEM((QUERY_HEADS // 2, tokens, HEAD_SIZE), bf16),
@@ -524,6 +576,8 @@
             dma((PLANES,)),
             dma((groups,)),
             dma((groups,)),
+            dma((2,)),
+            dma((2,)),
         ],
         compiler_params=pltpu.CompilerParams(
             collective_id=0, has_side_effects=True, vmem_limit_bytes=56 * 1024 * 1024

time: 44.5 us -> 43.1 us (0.969)
  Pallas kernels: 42.4 us -> 41 us
    pallas_call x1, Pallas kernels: 40.9 us -> 39.6 us  [packed_route(): pl.pallas_call(fused_kernel, out_shape=jax.ShapeDtypeStruct((tokens, widt...]
where the time goes in v6:
time: 43.1 us; the launch traced here: 42.9 us
  Pallas kernels  41 us (95%)
  local copies, waits for them, and re-layouts  0.97 us (2%)
  between operations  0.67 us (2%)
    pallas_call x1, Pallas kernels, packed_route(): pl.pallas_call(fused_kernel, out_shape=jax.ShapeDtypeStruct((tokens, widt...  39.6 us
    pallas_call x1, Pallas kernels, shards(): pl.pallas_call(fits_kernel, out_shape=jax.ShapeDtypeStruct((1,), jnp.int3...  1.45 us
    unnamed x1, local copies, waits for them, and re-layouts  0.97 us

profile of v6, /device:TPU:1, one launch (start us, length us, event | category | flops | bytes accessed | tf_op | source)
XLA Modules:
  0.0 42.9 jit_solution(12347278503958778784)
XLA Ops:
  0.0 1.5 %fits.1 = s32[1]{0:T(128)} custom-call(s32[8,128]{1,0:T(8,128)} %bitcast.72), custom_call_target="tpu_custom_call" | custom-call | tf_op jit(solution)/shard_map/fits/pallas_call | solution.py:610
  2.1 39.8 %conditional.1 = (bf16[128,4096]{1,0:T(8,128)(2,1)S(1)}) conditional(s32[]{:T(128)} %bitcast.20, (s32[1]{0:T(128)}, s32[1,8]{1,0:T(1,128)}, s32[1,8]{1,0:T(1,128)}, s32[128,8]{0,1:T(8,128)}, bf16[256,1,4096]{2,0,1:T(8,128)(2,1)}, /*index=5*/bf16[4096,512]{1,0:T(8,128)(2,1)}, bf16[4096,512]{1,0:T(8,128)(2,1)}, f32[128]{0:T(128)}, ...), branch_computations={%region_0.5_spmd, %region_5.6_spmd} | conditional | flops 4592182784 | bytes 141282944 | solution.py:617
  2.4 39.6 %fused_cross_attention.1 = bf16[128,4096]{1,0:T(8,128)(2,1)S(1)} custom-call(bf16[128,4096]{1,0:T(8,128)(2,1)} %get-tuple-element.58.q_hbm, bf16[256,4096]{1,0:T(8,128)(2,1)} %bitcast.68, bf16[4096,512]{1,0:T(8,128)(2,1)} %get-tuple-element.60.wk_hbm, bf16[4096,512]{1,0:T(8,128)(2,1)} %get-tuple-element.61.wv_hbm, f32[1,128]{1,0:T(1,128)} %bitcast.75, ...), custom_call_target="tpu_custom_call" | custom-call | tf_op jit(solution)/shard_map/cond/branch_1_fun/fused_cross_attention/pallas_call | solution.py:537
  41.9 1.0 %copy.116 = bf16[128,4096]{1,0:T(8,128)(2,1)} copy(bf16[128,4096]{1,0:T(8,128)(2,1)S(1)} %get-tuple-element.135) | data formatting | bytes 2097152

commit v7 on v6

--- a/solution.py
+++ b/solution.py
@@ -19,7 +19,7 @@
 MESH = pl.DeviceIdType.MESH
 MASKED = -32768.0
 PIECES = 8
-AHEAD = 3
+AHEAD = 6
 Z_STEPS = (0, 1, 7, 2, 6, 3, 5, 4)
 
 epsilon = 1e-05
@@ -114,13 +114,16 @@
     x_hbm,
     wk_hbm,
     wv_hbm,
-    qg_ref,
-    kg_ref,
+    qg_hbm,
+    kg_hbm,
     count_ref,
-    slot_ref,
+    slot_hbm,
     pos_ref,
     end_ref,
     out_hbm,
+    qg_ref,
+    kg_ref,
+    slot_ref,
     q_v,
     x_v,
     wk_v,
@@ -184,11 +187,18 @@
         hbm, v = ((wk_hbm, wk_v), (wv_hbm, wv_v))[i]
         return pltpu.make_async_copy(hbm.at[rows], v.at[rows], w_sem.at[i, c])
 
+    small = [
+        pltpu.make_async_copy(slot_hbm, slot_ref, local_sem.at[5]),
+        pltpu.make_async_copy(qg_hbm, qg_ref, local_sem.at[6]),
+        pltpu.make_async_copy(kg_hbm, kg_ref, local_sem.at[7]),
+    ]
+    for copy in small:
+        copy.start()
     for i in range(4):
         x_copy(i).start()
-    for c in range(AHEAD):
-        w_copy(0, c).start()
-        w_copy(1, c).start()
+    order = [(i, c) for i in range(2) for c in range(PIECES)]
+    for n in range(AHEAD):
+        w_copy(*order[n]).start()
 
     def z_to(s):
         return (z + Z_STEPS[s]) % PLANES
@@ -210,6 +220,9 @@
 
     lax.fori_loop(1, PLANES, greet_z, 0)
     lax.fori_loop(1, PLANE, greet_plane, 0)
+
+    for copy in small:
+        copy.wait()
 
     slots_t = slot_ref[...]
     present = slots_t >= 0
@@ -263,19 +276,6 @@
         iota((n_keys, HEAD_SIZE), 1) == iota((n_keys, HEAD_SIZE), 0) % IMG_MAX, MASKED, 0.0
     ).astype(jnp.bfloat16)
 
-    for i in range(4):
-        x_copy(i).wait()
-    for c in range(PIECES):
-        cols = pl.ds(c * piece, piece)
-        for i, (w, total) in enumerate(((wk_v, sum_k), (wv_v, sum_v))):
-            w_copy(i, c).wait()
-            if c + AHEAD < PIECES:
-                w_copy(i, c + AHEAD).start()
-            elif c + AHEAD == PIECES and i == 0:
-                q_copy.start()
-            term = mm(x_v[:, cols], w[cols, :])
-            total[...] = term if c == 0 else total[...] + term
-
     def part_copy(i):
         total, got = ((sum_k, got_k), (sum_v, got_v))[i]
         return pltpu.make_async_remote_copy(
@@ -287,8 +287,21 @@
             device_id_type=MESH,
         )
 
-    pl.semaphore_wait(barrier, PLANES - 1 + PLANE - 1 + 1)
-    part_copy(0).start()
+    for i in range(4):
+        x_copy(i).wait()
+    for n, (i, c) in enumerate(order):
+        w, total = ((wk_v, sum_k), (wv_v, sum_v))[i]
+        cols = pl.ds(c * piece, piece)
+        w_copy(i, c).wait()
+        if n + AHEAD < len(order):
+            w_copy(*order[n + AHEAD]).start()
+        elif n + AHEAD == len(order):
+            q_copy.start()
+        term = mm(x_v[:, cols], w[cols, :])
+        total[...] = term if c == 0 else total[...] + term
+        if (i, c) == (0, PIECES - 1):
+            pl.semaphore_wait(barrier, PLANES - 1 + PLANE - 1 + 1)
+            part_copy(0).start()
     part_copy(1).start()
 
     q_copy.wait()
@@ -528,7 +541,6 @@
     depth = vision.shape[2]
     two = 2 * HEAD_SIZE
     anywhere = pl.BlockSpec(memory_space=pl.ANY)
-    vmem = pl.BlockSpec(memory_space=pltpu.VMEM)
     smem = pl.BlockSpec(memory_space=pltpu.SMEM)
     bf16, f32 = jnp.bfloat16, jnp.float32
     dma = pltpu.SemaphoreType.DMA
@@ -537,9 +549,12 @@
     out = pl.pallas_call(
         fused_kernel,
         out_shape=jax.ShapeDtypeStruct((tokens, width), bf16),
-        in_specs=[anywhere, anywhere, anywhere, anywhere, vmem, vmem, smem, vmem, smem, smem],
+        in_specs=[anywhere] * 6 + [smem, anywhere, smem, smem],
         out_specs=anywhere,
         scratch_shapes=[
+            pltpu.VMEM((1, HEAD_SIZE), f32),
+            pltpu.VMEM((1, HEAD_SIZE), f32),
+            pltpu.VMEM((IMG_MAX, image_slot.shape[0]), jnp.int32),
             pltpu.VMEM((tokens, width), bf16),
             pltpu.VMEM((n_slots, depth), bf16),
             pltpu.VMEM(key_matrix.shape, bf16),
@@ -566,7 +581,7 @@
             pltpu.VMEM((GROUP, 4 * tokens, two), f32),
             pltpu.VMEM((tokens, width // 2), bf16),
             pltpu.VMEM((tokens, width // 2), bf16),
-            dma((5,)),
+            dma((8,)),
             dma((2, PIECES)),
             dma((4,)),
             dma((2, 2)),

time: 43.1 us -> 42.2 us (0.979)
  Pallas kernels: 41 us -> 40.2 us
    pallas_call x1, Pallas kernels: 39.6 us -> 38.7 us  [packed_route(): pl.pallas_call(fused_kernel, out_shape=jax.ShapeDtypeStruct((tokens, widt...]
where the time goes in v7:
time: 42.2 us; the launch traced here: 42 us
  Pallas kernels  40.2 us (95%)
  local copies, waits for them, and re-layouts  0.97 us (2%)
  between operations  0.67 us (2%)
    pallas_call x1, Pallas kernels, packed_route(): pl.pallas_call(fused_kernel, out_shape=jax.ShapeDtypeStruct((tokens, widt...  38.7 us
    pallas_call x1, Pallas kernels, shards(): pl.pallas_call(fits_kernel, out_shape=jax.ShapeDtypeStruct((1,), jnp.int3...  1.45 us
    unnamed x1, local copies, waits for them, and re-layouts  0.97 us

profile of v7, /device:TPU:1, one launch (start us, length us, event | category | flops | bytes accessed | tf_op | source)
XLA Modules:
  0.0 42.0 jit_solution(14135839822713137766)
XLA Ops:
  0.0 1.5 %fits.1 = s32[1]{0:T(128)} custom-call(s32[8,128]{1,0:T(8,128)} %bitcast.72), custom_call_target="tpu_custom_call" | custom-call | tf_op jit(solution)/shard_map/fits/pallas_call | solution.py:625
  2.1 38.9 %conditional.1 = (bf16[128,4096]{1,0:T(8,128)(2,1)S(1)}) conditional(s32[]{:T(128)} %bitcast.20, (s32[1]{0:T(128)}, s32[1,8]{1,0:T(1,128)}, s32[1,8]{1,0:T(1,128)}, s32[128,8]{0,1:T(8,128)}, bf16[256,1,4096]{2,0,1:T(8,128)(2,1)}, /*index=5*/bf16[4096,512]{1,0:T(8,128)(2,1)}, bf16[4096,512]{1,0:T(8,128)(2,1)}, f32[128]{0:T(128)}, ...), branch_computations={%region_0.5_spmd, %region_5.6_spmd} | conditional | flops 4592182784 | bytes 141282944 | solution.py:632
  2.4 38.7 %fused_cross_attention.1 = bf16[128,4096]{1,0:T(8,128)(2,1)S(1)} custom-call(bf16[128,4096]{1,0:T(8,128)(2,1)} %get-tuple-element.58.q_hbm, bf16[256,4096]{1,0:T(8,128)(2,1)} %bitcast.68, bf16[4096,512]{1,0:T(8,128)(2,1)} %get-tuple-element.60.wk_hbm, bf16[4096,512]{1,0:T(8,128)(2,1)} %get-tuple-element.61.wv_hbm, f32[1,128]{1,0:T(1,128)} %bitcast.75, ...), custom_call_target="tpu_custom_call" | custom-call | tf_op jit(solution)/shard_map/cond/branch_1_fun/fused_cross_attention/pallas_call | solution.py:549
  41.1 1.0 %copy.116 = bf16[128,4096]{1,0:T(8,128)(2,1)} copy(bf16[128,4096]{1,0:T(8,128)(2,1)S(1)} %get-tuple-element.135) | data formatting | bytes 2097152

commit v8 on v7

--- a/solution.py
+++ b/solution.py
@@ -364,7 +364,7 @@
     packed = mm(pick1[...], kv_own).astype(jnp.bfloat16).reshape(PLANES, CAPACITY, 2 * half)
     for s in range(1, PLANES):
         send1[s] = packed[s]
-    for s in range(1, PLANES):
+    for s in range(1, 5):
         hop1(s).start()
     def hop_one(n, i):
         return pltpu.make_async_remote_copy(
@@ -389,6 +389,8 @@
         lax.fori_loop(1, PLANE, body, 0)
 
     send_single(0, mm(pick_own[...], kv_own))
+    for s in range(5, PLANES):
+        hop1(s).start()
     pair = 2 * IMG_MAX
     rows_e, cols_e = PLANE * pair, 2 * CAPACITY
     row_rank = by_document(rank_plus, rows_e, pair)

time: 42.2 us -> 42.2 us (level)
  no operation moved by 1% of the time
where the time goes in v8:
time: 42.2 us; the launch traced here: 42 us
  Pallas kernels  40.2 us (95%)
  local copies, waits for them, and re-layouts  0.97 us (2%)
  between operations  0.67 us (2%)
    pallas_call x1, Pallas kernels, packed_route(): pl.pallas_call(fused_kernel, out_shape=jax.ShapeDtypeStruct((tokens, widt...  38.7 us
    pallas_call x1, Pallas kernels, shards(): pl.pallas_call(fits_kernel, out_shape=jax.ShapeDtypeStruct((1,), jnp.int3...  1.45 us
    unnamed x1, local copies, waits for them, and re-layouts  0.97 us

profile of v8, /device:TPU:1, one launch (start us, length us, event | category | flops | bytes accessed | tf_op | source)
XLA Modules:
  0.0 42.0 jit_solution(2708443698476559160)
XLA Ops:
  0.0 1.5 %fits.1 = s32[1]{0:T(128)} custom-call(s32[8,128]{1,0:T(8,128)} %bitcast.72), custom_call_target="tpu_custom_call" | custom-call | tf_op jit(solution)/shard_map/fits/pallas_call | solution.py:627
  2.1 38.9 %conditional.1 = (bf16[128,4096]{1,0:T(8,128)(2,1)S(1)}) conditional(s32[]{:T(128)} %bitcast.20, (s32[1]{0:T(128)}, s32[1,8]{1,0:T(1,128)}, s32[1,8]{1,0:T(1,128)}, s32[128,8]{0,1:T(8,128)}, bf16[256,1,4096]{2,0,1:T(8,128)(2,1)}, /*index=5*/bf16[4096,512]{1,0:T(8,128)(2,1)}, bf16[4096,512]{1,0:T(8,128)(2,1)}, f32[128]{0:T(128)}, ...), branch_computations={%region_0.5_spmd, %region_5.6_spmd} | conditional | flops 4592182784 | bytes 141282944 | solution.py:634
  2.4 38.7 %fused_cross_attention.1 = bf16[128,4096]{1,0:T(8,128)(2,1)S(1)} custom-call(bf16[128,4096]{1,0:T(8,128)(2,1)} %get-tuple-element.58.q_hbm, bf16[256,4096]{1,0:T(8,128)(2,1)} %bitcast.68, bf16[4096,512]{1,0:T(8,128)(2,1)} %get-tuple-element.60.wk_hbm, bf16[4096,512]{1,0:T(8,128)(2,1)} %get-tuple-element.61.wv_hbm, f32[1,128]{1,0:T(1,128)} %bitcast.75, ...), custom_call_target="tpu_custom_call" | custom-call | tf_op jit(solution)/shard_map/cond/branch_1_fun/fused_cross_attention/pallas_call | solution.py:551
  41.1 1.0 %copy.116 = bf16[128,4096]{1,0:T(8,128)(2,1)} copy(bf16[128,4096]{1,0:T(8,128)(2,1)S(1)} %get-tuple-element.135) | data formatting | bytes 2097152
